TPU v7x, 32 devices: a whole 2x2x4 slice. The times are simulated.
32 devices in a mesh: row: 4 (over x, core), seq: 8 (over z, y).
Axes of the slice: x: 2, y: 2, z: 4, core: 2. Of those that a mesh axis runs over, the one named last changes fastest.
Arguments:
- layer_input: float32 [8, 3072, 768], P('row', 'seq'), may hold values from -6 to 6
- doc_ids: int32 [8, 3072], P('row', 'seq'), may hold values from -1 to 1, as said below
- cotangent: float32 [8, 3072, 768], P('row', 'seq'), may hold values from -6 to 6
- attn_norm_gain: float32 [768], replicated, may hold values from 0.5 to 1.5
- attn_norm_bias: float32 [768], replicated, may hold values from -1.75 to 1.75
- query_weight: bfloat16 [768, 768], replicated, may hold values from -0.21875 to 0.21875
- query_bias: float32 [768], replicated, may hold values from -1.75 to 1.75
- key_weight: bfloat16 [768, 768], replicated, may hold values from -0.21875 to 0.21875
- value_weight: bfloat16 [768, 768], replicated, may hold values from -0.21875 to 0.21875
- value_bias: float32 [768], replicated, may hold values from -1.75 to 1.75
- output_weight: bfloat16 [768, 768], replicated, may hold values from -3.5 to 3.5
- output_bias: float32 [768], replicated, may hold values from -1.75 to 1.75
- feed_norm_gain: float32 [768], replicated, may hold values from 0.5 to 1.5
- feed_norm_bias: float32 [768], replicated, may hold values from -1.75 to 1.75
- up_weight: bfloat16 [768, 3072], replicated, may hold values from -0.21875 to 0.21875
- up_bias: float32 [3072], replicated, may hold values from -1.75 to 1.75
- down_weight: bfloat16 [3072, 768], replicated, may hold values from -0.109375 to 0.109375
- down_bias: float32 [768], replicated, may hold values from -1.75 to 1.75
Outputs:
- out: float32 [8, 3072, 768], P('row', 'seq')
- input_grad: float32 [8, 3072, 768], P('row', 'seq')
- grad_attn_norm_gain: float32 [768], P('seq')
- grad_attn_norm_bias: float32 [768], P('seq')
- grad_query_weight: float32 [768, 768], P('seq')
- grad_query_bias: float32 [768], P('seq')
- grad_key_weight: float32 [768, 768], P('seq')
- grad_value_weight: float32 [768, 768], P('seq')
- grad_value_bias: float32 [768], P('seq')
- grad_output_weight: float32 [768, 768], P('seq')
- grad_output_bias: float32 [768], P('seq')
- grad_feed_norm_gain: float32 [768], P('seq')
- grad_feed_norm_bias: float32 [768], P('seq')
- grad_up_weight: float32 [768, 3072], P('seq')
- grad_up_bias: float32 [3072], P('seq')
- grad_down_weight: float32 [3072, 768], P('seq')
- grad_down_bias: float32 [768], P('seq')
Inputs may be any that keep to these rules, and one draw needn't show every extreme that they name: `doc_ids`: in every packed row, document 0 fills the first 1 to 192 positions, document 1 runs from there until the padding, and padding (-1) fills the last 1 to 192 positions.
All inputs are finite; a program needn't handle non-finite values.
Results may differ from a plain program's by a relative error of at most 0.015.
Values may be sent and summed in bfloat16 or wider, within the bound.
No kernel may reach another device: no remote copies, remote signals or barrier semaphores. Data moves between devices by JAX's collectives and lax.ppermute only.
A program may use at most 512 MiB of HBM per device.

v0:
```python
import jax
import jax.numpy as jnp
from jax import lax
from jax.sharding import PartitionSpec as P

HEADS = 12
HEAD_DIM = 64
GROUP = 4
FIRST_DILATION = 1
SECOND_DILATION = 2
THIRD_DILATION = 4
FOURTH_DILATION = 6
FIFTH_DILATION = 12


EPS = 1e-05
NEG = -1e30
HIGH = lax.Precision.HIGHEST


def swapped(array, axis, apart):
    return lax.ppermute(array, axis, [(i, i ^ 1 << apart) for i in range(lax.axis_size(axis))])


def for_sending(array):

    def short(part):
        return part.astype(jnp.bfloat16) if part.dtype == jnp.float32 else part

    return jax.tree.map(short, array)


def layer_norm(values, gain, bias):
    center = values - jnp.mean(values, axis=-1, keepdims=True)
    spread = jnp.mean(center * center, axis=-1, keepdims=True)
    return center * lax.rsqrt(spread + EPS) * gain + bias


def project(inputs, weight):
    return jnp.einsum("ntd,df->ntf", inputs, weight, preferred_element_type=jnp.float32)


def project_back(grads, weight):
    return jnp.einsum("ntf,df->ntd", grads, weight, preferred_element_type=jnp.float32)


def weight_grad(inputs, grads):
    return jnp.einsum("ntd,ntf->df", inputs, grads, preferred_element_type=jnp.float32)


def column_sum(grads):
    return jnp.sum(grads.astype(jnp.float32), axis=(0, 1))


def pick_pairs(values, stride, picker):
    sequences, tokens, kinds, model_width = values.shape
    head_count = picker.shape[1]
    shaped = values.reshape(
        sequences, tokens // stride, stride, kinds, head_count, model_width // head_count
    )
    picked = jnp.einsum(
        "nsrche,rh->nsche", shaped, picker.astype(jnp.bfloat16), preferred_element_type=jnp.float32
    )
    return picked.astype(jnp.bfloat16).reshape(sequences, tokens // stride, kinds, model_width)


def spread_grads(values, stride, picker):
    sequences, slot_count, kinds, model_width = values.shape
    head_count = picker.shape[1]
    shaped = values.reshape(sequences, slot_count, kinds, head_count, model_width // head_count)
    spread = jnp.einsum("nsche,rh->nsrche", shaped, picker.astype(jnp.float32), precision=HIGH)
    return spread.reshape(sequences, slot_count * stride, kinds, model_width)


def group_gather(pieces, depth_list, device):
    gathered = list(pieces)
    for bit_index in range(max(depth_list)):
        active = [branch for branch in range(len(pieces)) if depth_list[branch] > bit_index]
        packed = jnp.concatenate([gathered[branch] for branch in active], 1)
        partner = swapped(packed, "seq", bit_index)
        lower = device // 2**bit_index % 2 == 0
        start = 0
        for branch in active:
            count = gathered[branch].shape[1]
            other = partner[:, start : start + count]
            start = start + count
            gathered[branch] = jnp.where(
                lower,
                jnp.concatenate((gathered[branch], other), 1),
                jnp.concatenate((other, gathered[branch]), 1),
            )
    return gathered


def group_return(pieces, depth_list, device):
    held = list(pieces)
    for bit_index in range(max(depth_list)):
        active = [branch for branch in range(len(pieces)) if depth_list[branch] > bit_index]
        lower = device // 2**bit_index % 2 == 0
        keep_parts = []
        send_parts = []
        for branch in active:
            sequences, count, kinds, model_width = held[branch].shape
            devices_left = 2 ** (depth_list[branch] - bit_index)
            slot_count = count // devices_left
            shaped = held[branch].reshape(
                sequences, devices_left // 2, 2, slot_count, kinds, model_width
            )
            even_part = shaped[:, :, 0].reshape(sequences, count // 2, kinds, model_width)
            odd_part = shaped[:, :, 1].reshape(sequences, count // 2, kinds, model_width)
            keep_parts.append(jnp.where(lower, even_part, odd_part))
            send_parts.append(jnp.where(lower, odd_part, even_part))
        received = swapped(for_sending(jnp.concatenate(send_parts, 1)), "seq", bit_index)
        start = 0
        for branch, kept in zip(active, keep_parts):
            count = kept.shape[1]
            held[branch] = kept + received[:, start : start + count]
            start = start + count
    return held


def per_device(
    layer_input,
    doc_ids,
    cotangent,
    attn_norm_gain,
    attn_norm_bias,
    query_weight,
    query_bias,
    key_weight,
    value_weight,
    value_bias,
    output_weight,
    output_bias,
    feed_norm_gain,
    feed_norm_bias,
    up_weight,
    up_bias,
    down_weight,
    down_bias,
):
    sequences, tokens, model_width = layer_input.shape
    head_count = HEADS
    head_size = HEAD_DIM
    score_scale = head_size ** (-0.5)
    device = lax.axis_index("seq")
    axis_count = lax.axis_size("seq")
    branch_strides = (
        FIRST_DILATION,
        SECOND_DILATION,
        THIRD_DILATION,
        FOURTH_DILATION,
        FIFTH_DILATION,
    )
    group_sizes = tuple((min(GROUP * 2**branch, axis_count) for branch in range(5)))
    depth_list = tuple((group_size.bit_length() - 1 for group_size in group_sizes))
    slot_counts = tuple((tokens // stride for stride in branch_strides))
    pickers = tuple(
        (
            jnp.arange(stride)[:, None] == jnp.arange(head_count)[None, :] % stride
            for stride in branch_strides
        )
    )
    docs_all = lax.all_gather(doc_ids, "seq", axis=1, tiled=True)
    segment_docs = []
    for branch in range(5):
        group_size = group_sizes[branch]
        group_start = device // group_size * group_size * tokens
        segment_docs.append(lax.dynamic_slice_in_dim(docs_all, group_start, group_size * tokens, 1))
    masked_grad = jnp.where((doc_ids >= 0)[..., None], cotangent, 0.0)
    h_first = layer_norm(layer_input, attn_norm_gain, attn_norm_bias).astype(jnp.bfloat16)
    query_low = (project(h_first, query_weight) + query_bias).astype(jnp.bfloat16)
    key_low = project(h_first, key_weight).astype(jnp.bfloat16)
    value_low = (project(h_first, value_weight) + value_bias).astype(jnp.bfloat16)
    pairs_low = jnp.stack((key_low, value_low), 2)
    own_sets = [
        pick_pairs(pairs_low, branch_strides[branch], pickers[branch]) for branch in range(5)
    ]
    gathered_sets = group_gather(own_sets, depth_list, device)

    def branch_scores(head_index, branch):
        stride = branch_strides[branch]
        group_size = group_sizes[branch]
        slot_count = slot_counts[branch]
        offset = head_index % stride
        chosen = jnp.arange(stride) == offset
        query_head = lax.dynamic_slice_in_dim(query_low, head_index * head_size, head_size, 2)
        query_sel = lax.dynamic_index_in_dim(
            query_head.reshape(sequences, slot_count, stride, head_size), offset, 2, keepdims=False
        )
        key_sel = lax.dynamic_slice_in_dim(
            gathered_sets[branch][:, :, 0], head_index * head_size, head_size, 2
        )
        value_sel = lax.dynamic_slice_in_dim(
            gathered_sets[branch][:, :, 1], head_index * head_size, head_size, 2
        )
        key_docs = lax.dynamic_index_in_dim(
            segment_docs[branch].reshape(sequences, group_size * slot_count, stride),
            offset,
            2,
            keepdims=False,
        )
        query_docs = lax.dynamic_index_in_dim(
            doc_ids.reshape(sequences, slot_count, stride), offset, 2, keepdims=False
        )
        key_index = jnp.arange(group_size * slot_count, dtype=jnp.int32)
        query_index = device % group_size * slot_count + jnp.arange(slot_count, dtype=jnp.int32)
        mask = (key_index[None, None, :] <= query_index[None, :, None]) & (
            key_docs[:, None, :] == query_docs[:, :, None]
        )
        score = jnp.where(
            mask,
            score_scale
            * jnp.einsum("nqe,nke->nqk", query_sel, key_sel, preferred_element_type=jnp.float32),
            NEG,
        )
        return (chosen, offset, query_sel, key_sel, value_sel, score)

    def head_forward(head_index):
        found = [branch_scores(head_index, branch) for branch in range(5)]
        total = jnp.full((sequences, tokens), NEG, dtype=jnp.float32)
        for branch in range(5):
            chosen, offset, query_sel, key_sel, value_sel, score = found[branch]
            part_total = jax.nn.logsumexp(score, axis=-1)
            spread = jnp.where(chosen, part_total[..., None], NEG).reshape(sequences, tokens)
            total = jnp.logaddexp(total, spread)
        result = jnp.zeros((sequences, tokens, head_size), dtype=jnp.float32)
        for branch in range(5):
            chosen, offset, query_sel, key_sel, value_sel, score = found[branch]
            stride = branch_strides[branch]
            total_sel = lax.dynamic_index_in_dim(
                total.reshape(sequences, slot_counts[branch], stride), offset, 2, keepdims=False
            )
            prob = jnp.exp(score - total_sel[..., None]).astype(jnp.bfloat16)
            part = jnp.einsum("nqk,nke->nqe", prob, value_sel, preferred_element_type=jnp.float32)
            result = result + jnp.where(chosen[:, None], part[:, :, None, :], 0.0).reshape(
                sequences, tokens, head_size
            )
        return (result, total)

    head_outs, totals = lax.map(head_forward, jnp.arange(head_count, dtype=jnp.int32))
    attended = (
        head_outs.transpose(1, 2, 0, 3).reshape(sequences, tokens, model_width).astype(jnp.bfloat16)
    )
    middle = layer_input + project(attended, output_weight) + output_bias
    h_second = layer_norm(middle, feed_norm_gain, feed_norm_bias).astype(jnp.bfloat16)
    hidden = project(h_second, up_weight) + up_bias
    active_full, gelu_pull = jax.vjp(jax.nn.gelu, hidden)
    active = active_full.astype(jnp.bfloat16)
    result_out = middle + project(active, down_weight) + down_bias
    down_grad = masked_grad.astype(jnp.bfloat16)
    grad_down_weight = weight_grad(active, down_grad)
    grad_down_bias = column_sum(down_grad)
    active_grad = jnp.einsum(
        "ntd,fd->ntf", down_grad, down_weight, preferred_element_type=jnp.float32
    )
    hidden_grad = gelu_pull(active_grad)[0].astype(jnp.bfloat16)
    grad_up_weight = weight_grad(h_second, hidden_grad)
    grad_up_bias = column_sum(hidden_grad)
    norm_input_grad = project_back(hidden_grad, up_weight)
    norm_pull = jax.vjp(layer_norm, middle, feed_norm_gain, feed_norm_bias)[1]
    middle_part, grad_feed_norm_gain, grad_feed_norm_bias = norm_pull(norm_input_grad)
    middle_grad = masked_grad + middle_part
    branch_grad = middle_grad.astype(jnp.bfloat16)
    grad_output_weight = weight_grad(attended, branch_grad)
    grad_output_bias = column_sum(branch_grad)
    attended_grad = project_back(branch_grad, output_weight).astype(jnp.bfloat16)

    def head_backward(item):
        head_index, total = item
        found = [branch_scores(head_index, branch) for branch in range(5)]
        out_grad = lax.dynamic_slice_in_dim(attended_grad, head_index * head_size, head_size, 2)
        balance = jnp.zeros((sequences, tokens), dtype=jnp.float32)
        kept = []
        for branch in range(5):
            chosen, offset, query_sel, key_sel, value_sel, score = found[branch]
            stride = branch_strides[branch]
            slot_count = slot_counts[branch]
            total_sel = lax.dynamic_index_in_dim(
                total.reshape(sequences, slot_count, stride), offset, 2, keepdims=False
            )
            grad_sel = lax.dynamic_index_in_dim(
                out_grad.reshape(sequences, slot_count, stride, head_size),
                offset,
                2,
                keepdims=False,
            )
            prob = jnp.exp(score - total_sel[..., None])
            flow = jnp.einsum(
                "nqe,nke->nqk", grad_sel, value_sel, preferred_element_type=jnp.float32
            )
            balance = balance + jnp.where(
                chosen, jnp.sum(prob * flow, axis=-1)[..., None], 0.0
            ).reshape(sequences, tokens)
            kept.append((prob, flow, grad_sel))
        query_part = jnp.zeros((sequences, tokens, head_size), dtype=jnp.float32)
        key_parts = []
        for branch in range(5):
            chosen, offset, query_sel, key_sel, value_sel, score = found[branch]
            prob, flow, grad_sel = kept[branch]
            stride = branch_strides[branch]
            balance_sel = lax.dynamic_index_in_dim(
                balance.reshape(sequences, slot_counts[branch], stride), offset, 2, keepdims=False
            )
            slope = (prob * (flow - balance_sel[..., None])).astype(jnp.bfloat16)
            part = score_scale * jnp.einsum(
                "nqk,nke->nqe", slope, key_sel, preferred_element_type=jnp.float32
            )
            query_part = query_part + jnp.where(chosen[:, None], part[:, :, None, :], 0.0).reshape(
                sequences, tokens, head_size
            )
            key_term = score_scale * jnp.einsum(
                "nqk,nqe->nke", slope, query_sel, preferred_element_type=jnp.float32
            )
            value_term = jnp.einsum(
                "nqk,nqe->nke",
                prob.astype(jnp.bfloat16),
                grad_sel,
                preferred_element_type=jnp.float32,
            )
            key_parts.append(jnp.stack((key_term, value_term), 2))
        return (query_part, balance, tuple(key_parts))

    query_heads, balances, far_parts = lax.map(
        head_backward, (jnp.arange(head_count, dtype=jnp.int32), totals)
    )
    returned_sets = []
    for branch in range(5):
        shaped = far_parts[branch].transpose(1, 2, 3, 0, 4)
        returned_sets.append(shaped.reshape(sequences, shaped.shape[1], 2, model_width))
    owned = group_return(returned_sets, depth_list, device)
    pair_grad = spread_grads(owned[0], branch_strides[0], pickers[0])
    for branch in range(1, 5):
        pair_grad = pair_grad + spread_grads(owned[branch], branch_strides[branch], pickers[branch])
    key_grad = pair_grad[:, :, 0].astype(jnp.bfloat16)
    value_grad = pair_grad[:, :, 1].astype(jnp.bfloat16)
    query_grad = (
        query_heads.transpose(1, 2, 0, 3)
        .reshape(sequences, tokens, model_width)
        .astype(jnp.bfloat16)
    )
    grad_query_weight = weight_grad(h_first, query_grad)
    grad_query_bias = column_sum(query_grad)
    grad_key_weight = weight_grad(h_first, key_grad)
    grad_value_weight = weight_grad(h_first, value_grad)
    grad_value_bias = column_sum(value_grad)
    first_grad = (
        project_back(query_grad, query_weight)
        + project_back(key_grad, key_weight)
        + project_back(value_grad, value_weight)
    )
    first_pull = jax.vjp(layer_norm, layer_input, attn_norm_gain, attn_norm_bias)[1]
    input_part, grad_attn_norm_gain, grad_attn_norm_bias = first_pull(first_grad)
    input_grad = middle_grad + input_part
    summed = (
        lax.psum_scatter(grad_attn_norm_gain, "seq", scatter_dimension=0, tiled=True),
        lax.psum_scatter(grad_attn_norm_bias, "seq", scatter_dimension=0, tiled=True),
        lax.psum_scatter(grad_query_weight, "seq", scatter_dimension=0, tiled=True),
        lax.psum_scatter(grad_query_bias, "seq", scatter_dimension=0, tiled=True),
        lax.psum_scatter(grad_key_weight, "seq", scatter_dimension=0, tiled=True),
        lax.psum_scatter(grad_value_weight, "seq", scatter_dimension=0, tiled=True),
        lax.psum_scatter(grad_value_bias, "seq", scatter_dimension=0, tiled=True),
        lax.psum_scatter(grad_output_weight, "seq", scatter_dimension=0, tiled=True),
        lax.psum_scatter(grad_output_bias, "seq", scatter_dimension=0, tiled=True),
        lax.psum_scatter(grad_feed_norm_gain, "seq", scatter_dimension=0, tiled=True),
        lax.psum_scatter(grad_feed_norm_bias, "seq", scatter_dimension=0, tiled=True),
        lax.psum_scatter(grad_up_weight, "seq", scatter_dimension=0, tiled=True),
        lax.psum_scatter(grad_up_bias, "seq", scatter_dimension=0, tiled=True),
        lax.psum_scatter(grad_down_weight, "seq", scatter_dimension=0, tiled=True),
        lax.psum_scatter(grad_down_bias, "seq", scatter_dimension=0, tiled=True),
    )
    final = (
        lax.psum(summed[0].astype(jnp.bfloat16), "row").astype(jnp.float32),
        lax.psum(summed[1].astype(jnp.bfloat16), "row").astype(jnp.float32),
        lax.psum(summed[2].astype(jnp.bfloat16), "row").astype(jnp.float32),
        lax.psum(summed[3].astype(jnp.bfloat16), "row").astype(jnp.float32),
        lax.psum(summed[4].astype(jnp.bfloat16), "row").astype(jnp.float32),
        lax.psum(summed[5].astype(jnp.bfloat16), "row").astype(jnp.float32),
        lax.psum(summed[6].astype(jnp.bfloat16), "row").astype(jnp.float32),
        lax.psum(summed[7].astype(jnp.bfloat16), "row").astype(jnp.float32),
        lax.psum(summed[8].astype(jnp.bfloat16), "row").astype(jnp.float32),
        lax.psum(summed[9].astype(jnp.bfloat16), "row").astype(jnp.float32),
        lax.psum(summed[10].astype(jnp.bfloat16), "row").astype(jnp.float32),
        lax.psum(summed[11].astype(jnp.bfloat16), "row").astype(jnp.float32),
        lax.psum(summed[12].astype(jnp.bfloat16), "row").astype(jnp.float32),
        lax.psum(summed[13].astype(jnp.bfloat16), "row").astype(jnp.float32),
        lax.psum(summed[14].astype(jnp.bfloat16), "row").astype(jnp.float32),
    )
    return (
        result_out,
        input_grad,
        final[0],
        final[1],
        final[2],
        final[3],
        final[4],
        final[5],
        final[6],
        final[7],
        final[8],
        final[9],
        final[10],
        final[11],
        final[12],
        final[13],
        final[14],
    )


def solution(mesh):
    placed = (
        P("row", "seq", None),
        P("row", "seq"),
        P("row", "seq", None),
        P(),
        P(),
        P(),
        P(),
        P(),
        P(),
        P(),
        P(),
        P(),
        P(),
        P(),
        P(),
        P(),
        P(),
        P(),
    )
    return jax.shard_map(
        per_device,
        mesh=mesh,
        in_specs=placed,
        out_specs=(
            P("row", "seq", None),
            P("row", "seq", None),
            P("seq"),
            P("seq"),
            P("seq", None),
            P("seq"),
            P("seq", None),
            P("seq", None),
            P("seq"),
            P("seq", None),
            P("seq"),
            P("seq"),
            P("seq"),
            P("seq", None),
            P("seq"),
            P("seq", None),
            P("seq"),
        ),
        check_vma=False,
    )
```

profile of v0, /device:TPU:1, one launch (start us, length us, event | category | flops | bytes accessed | tf_op | source)
XLA Modules:
  0.0 6047.1 jit_solution(13586292234723673667)
XLA Ops:
  92.6 101.9 %collective-permute-done = bf16[2,768,2,768]{1,3,0,2:T(8,128)(2,1)} collective-permute-done((bf16[2,768,2,768]{1,3,0,2:T(8,128)(2,1)}, bf16[2,768,2,768]{1,3,0,2:T(8,128)(2,1)}, u32[]{:S(2)}, u32[]{:S(2)}) %collective-permute-start) | collective-permute-done | bytes 4718624 | tf_op jit(solution)/shard_map/ppermute | solution.py:22
  216.2 14.5 concatenate.121
  231.9 202.3 %collective-permute-done.1 = bf16[2,1536,2,768]{1,3,0,2:T(8,128)(2,1)} collective-permute-done((bf16[2,1536,2,768]{1,3,0,2:T(8,128)(2,1)}, bf16[2,1536,2,768]{1,3,0,2:T(8,128)(2,1)}, u32[]{:S(2)}, u32[]{:S(2)}) %collective-permute-start.1) | collective-permute-done | bytes 9437216 | tf_op jit(solution)/shard_map/ppermute | solution.py:22
  461.2 418.5 %all_gather.3 = s32[2,3072]{1,0:T(2,128)S(1)} all-gather(s32[2,384]{1,0:T(2,128)S(1)} %copy-done.93), channel_id=1, replica_groups=mesh['row'=4,'seq'=8] {'seq'}, dimensions={1}, use_global_device_ids=true | all-gather | bytes 27648 | tf_op jit(solution)/shard_map/all_gather | solution.py:164
  913.9 1481.4 %while.44 = (s32[]{:T(128)}, bf16[12,2,384,64]{2,3,0,1:T(8,128)(2,1)}, f32[12,2,384]{2,1,0:T(2,128)}, s32[]{:T(128)}, s32[2,1536]{1,0:T(2,128)}, /*index=5*/s32[...) while((s32[]{:T(128)}, ...), condition=%wide.region_13.14_spmd, body=%wide.region_2.13_spmd.sunk | while | flops 531293312 | bytes 129217016 | solution.py:241
  976.6 13.0 fusion.406
  1100.0 13.0 fusion.406
  1470.2 13.0 fusion.406
  2437.4 2068.8 %while.45 = (s32[]{:T(128)}, bf16[12,2,384,64]{2,3,0,1:T(8,128)(2,1)}, f32[12,2,1536,2,64]{2,4,1,3,0:T(8,128)}, f32[12,2,1536,2,64]{2,4,1,3,0:T(8,128)}, f32[12,...) while((s32[]{:T(128)}, ...), condition=%wide.region_24.25_spmd, body=%wide.region_18.24_spmd.sunk | while | flops 1304522112 | bytes 263599216 | solution.py:324
  4518.8 22.2 reshape_reshape.15
  4547.7 14.1 reshape_reshape.18
  4561.8 17.1 fusion.208
  4606.7 15.2 copy.536
  4621.8 15.2 copy.535
  4640.6 22.3 copy.433
  4671.3 19.2 reshape_reshape.17
  4703.2 32.7 reshape_reshape.16
  4738.4 27.0 fusion.273
  4765.4 15.9 fusion.275
  4781.3 15.6 copy.534
  4796.9 15.6 copy.533
  4815.6 29.8 copy.532
  4845.4 29.8 copy.531
  4911.7 18.0 broadcast_select_fusion.5
  4929.6 23.3 copy.523
  4977.0 284.0 %collective-permute-done.3 = bf16[2,2304,2,768]{3,1,2,0:T(8,128)(2,1)} collective-permute-done((bf16[2,2304,2,768]{3,1,2,0:T(8,128)(2,1)}, bf16[2,2304,2,768]{3,1,2,0:T(8,128)(2,1)}, u32[]{:S(2)}, u32[]{:S(2)}) %collective-permute-start.3) | collective-permute-done | bytes 14155808 | tf_op jit(solution)/shard_map/ppermute | solution.py:22
  5317.6 229.9 %collective-permute-done.4 = bf16[2,1152,2,768]{3,1,2,0:T(8,128)(2,1)} collective-permute-done((bf16[2,1152,2,768]{3,1,2,0:T(8,128)(2,1)}, bf16[2,1152,2,768]{3,1,2,0:T(8,128)(2,1)}, u32[]{:S(2)}, u32[]{:S(2)}) %collective-permute-start.4) | collective-permute-done | bytes 7077920 | tf_op jit(solution)/shard_map/ppermute | solution.py:22
  5599.2 103.6 %collective-permute-done.5 = bf16[2,384,2,768]{1,3,2,0:T(8,128)(2,1)S(1)} collective-permute-done((bf16[2,384,2,768]{1,3,2,0:T(8,128)(2,1)S(1)}, bf16[2,384,2,768]{1,3,2,0:T(8,128)(2,1)S(1)}, u32[]{:S(2)}, u32[]{:S(2)}) %collective-permute-start.5) | collective-permute-done | bytes 2359328 | tf_op jit(solution)/shard_map/ppermute | solution.py:22
  5859.8 23.8 reduce-scatter.11.cloned.1.call-done
  5885.2 69.8 %reduce-scatter.9.cloned.1.call-done = f32[96,768]{1,0:T(8,128)} async-done(((f32[768,768]{1,0:T(8,128)}), f32[96,768]{1,0:T(8,128)}) %reduce-scatter.9.cloned.1.call-update) | async-done | bytes 294928 | tf_op jit(solution)/shard_map/reduce_scatter | solution.py:360
  5958.7 29.3 all-reduce.9
  5999.5 14.7 all-reduce.10
  (7557 shorter events, 4049.3 us)
Async XLA Ops:
  7.2 5836.6 %reduce-scatter.13.cloned.1.call-start = ((), (), s32[]{:S(2)}) async-start(), calls=%async_computation.9 | async-start | bytes 2654208 | tf_op jit(solution)/shard_map/reduce_scatter | solution.py:363
  90.5 103.9 %collective-permute-start = (bf16[2,768,2,768]{1,3,0,2:T(8,128)(2,1)}, bf16[2,768,2,768]{1,3,0,2:T(8,128)(2,1)}, u32[]{:S(2)}, u32[]{:S(2)}) collective-permute-start(bf16[2,768,2,768]{1,3,0,2:T(8,128)(2,1)} %concatenate.110), channel_id=1, source_target_pairs={{0,1},{1,0},{2,3},{3,2},{4,5},{5,4},{6,7},{7,6},{8,9},{9,8},{10,11... | collective-permute-start | bytes 14155784 | tf_op jit(solution)/shard_map/ppermute | solution.py:22
  230.7 203.5 %collective-permute-start.1 = (bf16[2,1536,2,768]{1,3,0,2:T(8,128)(2,1)}, bf16[2,1536,2,768]{1,3,0,2:T(8,128)(2,1)}, u32[]{:S(2)}, u32[]{:S(2)}) collective-permute-start(bf16[2,1536,2,768]{1,3,0,2:T(8,128)(2,1)} %concatenate.121), channel_id=1, source_target_pairs={{0,2},{1,3},{2,0},{3,1},{4,6},{5,7},{6,4},{7,5},{8,10},{9,11},{10,... | collective-permute-start | bytes 28311560 | tf_op jit(solution)/shard_map/ppermute | solution.py:22
  455.5 436.9 %collective-permute-start.2 = (bf16[2,1536,2,768]{1,3,0,2:T(8,128)(2,1)}, bf16[2,1536,2,768]{1,3,0,2:T(8,128)(2,1)}, u32[]{:S(2)}, u32[]{:S(2)}) collective-permute-start(bf16[2,1536,2,768]{1,3,0,2:T(8,128)(2,1)} %fusion.200), channel_id=1, source_target_pairs={{0,4},{1,5},{2,6},{3,7},{4,0},{5,1},{6,2},{7,3},{8,12},{9,13},{10,... | collective-permute-start | bytes 28311560 | tf_op jit(solution)/shard_map/ppermute | solution.py:22
  2436.2 3409.3 %reduce-scatter.7.cloned.1.call-start = ((), (), s32[]{:S(2)}) async-start(), calls=%async_computation.6 | async-start | bytes 2654208 | tf_op jit(solution)/shard_map/reduce_scatter | solution.py:358
  2437.6 44.4 copy-start.29
  2437.6 56.1 copy-start.6
  2610.0 56.1 copy-start.6
  2782.3 56.1 copy-start.6
  2954.6 56.1 copy-start.6
  3127.0 56.1 copy-start.6
  3299.4 44.4 copy-start.29
  3299.4 56.1 copy-start.6
  3471.8 56.1 copy-start.6
  3644.1 56.1 copy-start.6
  3816.4 56.1 copy-start.6
  3988.8 44.4 copy-start.29
  3988.8 56.1 copy-start.6
  4161.2 56.1 copy-start.6
  4333.5 44.4 copy-start.29
  4333.5 56.1 copy-start.6
  4765.4 1081.8 %reduce-scatter.17.cloned.1.call-start = ((), (), s32[]{:S(2)}) async-start(), calls=%async_computation.11 | async-start | bytes 10616832 | tf_op jit(solution)/shard_map/reduce_scatter | solution.py:369
  4898.0 363.0 %collective-permute-start.3 = (bf16[2,2304,2,768]{3,1,2,0:T(8,128)(2,1)}, bf16[2,2304,2,768]{3,1,2,0:T(8,128)(2,1)}, u32[]{:S(2)}, u32[]{:S(2)}) collective-permute-start(bf16[2,2304,2,768]{3,1,2,0:T(8,128)(2,1)} %constant_dynamic-update-slice_fusion.1), channel_id=1, source_target_pairs={{0,1},{1,0},{2,3},{3,2},{4,5},{5,4},{6,7},{7,6},{8,9},{9,8},{10,11... | collective-permute-start | bytes 42467336 | tf_op jit(solution)/shard_map/ppermute | solution.py:22
  4906.9 942.4 %reduce-scatter.15.cloned.1.call-start = ((), (), s32[]{:S(2)}) async-start(), calls=%async_computation.10 | async-start | bytes 10616832 | tf_op jit(solution)/shard_map/reduce_scatter | solution.py:367
  5295.5 251.9 %collective-permute-start.4 = (bf16[2,1152,2,768]{3,1,2,0:T(8,128)(2,1)}, bf16[2,1152,2,768]{3,1,2,0:T(8,128)(2,1)}, u32[]{:S(2)}, u32[]{:S(2)}) collective-permute-start(bf16[2,1152,2,768]{3,1,2,0:T(8,128)(2,1)} %constant_dynamic-update-slice_fusion.6), channel_id=1, source_target_pairs={{0,2},{1,3},{2,0},{3,1},{4,6},{5,7},{6,4},{7,5},{8,10},{9,11},{10,... | collective-permute-start | bytes 21233672 | tf_op jit(solution)/shard_map/ppermute | solution.py:22
  5302.6 580.9 %reduce-scatter.11.cloned.1.call-start = ((), (), s32[]{:S(2)}) async-start(), calls=%async_computation.8 | async-start | bytes 2654208 | tf_op jit(solution)/shard_map/reduce_scatter | solution.py:361
  5597.8 105.0 %copy-start.65 = (f32[2,1,1,32,2,768]{3,5,4,0,2,1:T(8,128)S(1)}, f32[2,1,1,32,2,768]{3,5,4,0,2,1:T(8,128)}, u32[]{:S(2)}) copy-start(f32[2,1,1,32,2,768]{3,5,4,0,2,1:T(8,128)} %copy.544) | copy-start | bytes 1179652
  5597.8 104.9 %copy-start.66 = (f32[2,1,1,32,2,768]{3,5,4,0,2,1:T(8,128)S(1)}, f32[2,1,1,32,2,768]{3,5,4,0,2,1:T(8,128)}, u32[]{:S(2)}) copy-start(f32[2,1,1,32,2,768]{3,5,4,0,2,1:T(8,128)} %copy.545) | copy-start | bytes 1179652
  5599.1 103.7 %collective-permute-start.5 = (bf16[2,384,2,768]{1,3,2,0:T(8,128)(2,1)S(1)}, bf16[2,384,2,768]{1,3,2,0:T(8,128)(2,1)S(1)}, u32[]{:S(2)}, u32[]{:S(2)}) collective-permute-start(bf16[2,384,2,768]{1,3,2,0:T(8,128)(2,1)S(1)} %pad_maximum_fusion.3), channel_id=1, source_target_pairs={{0,4},{1,5},{2,6},{3,7},{4,0},{5,1},{6,2},{7,3},{8,12},{9,13},{10,... | collective-permute-start | bytes 7077896 | tf_op jit(solution)/shard_map/ppermute | solution.py:22
  5818.2 136.8 %reduce-scatter.9.cloned.1.call-start = ((), (), s32[]{:S(2)}) async-start(), calls=%async_computation.7 | async-start | bytes 2654208 | tf_op jit(solution)/shard_map/reduce_scatter | solution.py:360
  5822.5 207.5 %all-reduce.14.cloned.1.call-start = ((), (), s32[]{:S(2)}) async-start(), calls=%async_computation.12 | async-start | bytes 3538944 | tf_op jit(solution)/shard_map/psum | solution.py:375
  5859.8 165.6 %copy-start.175 = (f32[2,384]{1,0:T(2,128)S(1)}, f32[2,384]{1,0:T(2,128)}, u32[]{:S(2)}) copy-start(f32[2,384]{1,0:T(2,128)} %copy-done.174) | copy-start | bytes 9220
  (1468 other events, 8384.2 us)
Sparse Core Ops, SparseCore 0:
  2436.3 70.7 reduce-scatter.12
  4765.5 70.6 reduce-scatter.6
  4907.0 203.0 reduce-scatter.16
  5302.7 260.4 reduce-scatter.14
  5818.3 65.2 reduce-scatter.10
  5886.9 68.0 reduce-scatter.8
  5959.0 46.7 all-reduce.13
where the time goes:
time: 6100 us; the launch traced here: 6050 us
  local copies, waits for them, and re-layouts  2990 us (49%)
  waiting for transfers between devices  1020 us (17%)
  other arithmetic  787 us (13%)
  matrix products  651 us (11%)
  blocking collectives  462 us (8%)
  loops' own time  117 us (2%)
    ppermute x6, waiting for transfers between devices, swapped(): lax.ppermute(array, axis, [(i, i ^ 1 << apart) for i in range(lax.axis_si...  922 us
    slice x108, local copies, waits for them, and re-layouts, branch_scores(): gathered_sets[branch][:, :, 1]  473 us
    all_gather x1, blocking collectives, per_device(): docs_all = lax.all_gather(doc_ids, 'seq', axis=1, tiled=True)  418 us
    broadcast_in_dim x756, local copies, waits for them, and re-layouts, head_forward(): jnp.where(chosen, part_total[..., None], NEG).reshape(sequences, tokens)  383 us
    broadcast_in_dim x708, local copies, waits for them, and re-layouts, head_backward(): jnp.where(chosen, jnp.sum(prob * flow, axis=-1)[..., None], 0.0)  254 us
    unnamed x245, local copies, waits for them, and re-layouts  197 us
    broadcast_in_dim x96, local copies, waits for them, and re-layouts, head_backward(): jnp.where(chosen[:, None], part[:, :, None, :], 0.0)  170 us
    reshape x96, local copies, waits for them, and re-layouts, branch_scores(): segment_docs[branch].reshape(sequences, group_size * slot_count, stride)  138 us

commit v1 on v0

--- a/solution.py
+++ b/solution.py
@@ -1,6 +1,11 @@
+import functools
+import math
+
 import jax
 import jax.numpy as jnp
 from jax import lax
+from jax.experimental import pallas as pl
+from jax.experimental.pallas import tpu as pltpu
 from jax.sharding import PartitionSpec as P
 
 HEADS = 12
@@ -407,6 +412,768 @@
     )
 
 
+TOK = 384
+HALF = TOK // 2
+BLOCKS = 8
+LEN = TOK * BLOCKS
+SEG = LEN // 2
+PAR = SEG // 2
+TILE = 256
+TILES = PAR // TILE
+OWN_HEADS = 3
+WIDTH = OWN_HEADS * HEAD_DIM
+FAR = -1e9
+LOG2E = math.log2(math.e)
+BOTH = ("row", "seq")
+VMEM_LIMIT = 56 * 1024 * 1024
+
+
+def permutation(move):
+    pairs = []
+    for x in range(2):
+        for core in range(2):
+            for z in range(4):
+                for y in range(2):
+                    core_to, z_to, y_to, x_to = move(core, z, y, x)
+                    source = (2 * x + core) * 8 + 2 * z + y
+                    pairs.append((source, (2 * x_to + core_to) * 8 + 2 * z_to + y_to))
+    return pairs
+
+
+def inverse(pairs):
+    return sorted((b, a) for a, b in pairs)
+
+
+def send(array, pairs):
+    return lax.ppermute(array, BOTH, pairs)
+
+
+def to_row(slot):
+    return permutation(lambda core, z, y, x: (z >> 1, 2 * core + (slot ^ (z & 1)), y, x))
+
+
+SWAP_CORE = permutation(lambda core, z, y, x: (1 - core, z, y, x))
+SWAP_X = permutation(lambda core, z, y, x: (core, z, y, 1 - x))
+SWAP_Y = permutation(lambda core, z, y, x: (core, z, 1 - y, x))
+SWAP_Z_LOW = permutation(lambda core, z, y, x: (core, z ^ 1, y, x))
+SWAP_Z_HIGH = permutation(lambda core, z, y, x: (core, z ^ 2, y, x))
+
+
+def to_owner(delta):
+    high, low, side = delta >> 2, delta >> 1 & 1, delta & 1
+    return permutation(
+        lambda core, z, y, x: (z >> 1, 2 * (core ^ high) + ((z & 1) ^ low), y ^ side, x)
+    )
+
+
+def pick(bit, zero, one):
+    return jnp.where(bit == 0, zero, one)
+
+
+def halves(array, bit, axis=0):
+    first, second = jnp.split(array, 2, axis)
+    return pick(bit, first, second), pick(bit, second, first)
+
+
+def joined(mine, other, bit, axis=0):
+    return jnp.concatenate((pick(bit, mine, other), pick(bit, other, mine)), axis)
+
+
+def columns(width):
+    return [(part, slice(128 * part, 128 * (part + 1))) for part in range(width // 128)]
+
+
+def read_sorted(in_ref, lanes):
+    for part, column in columns(in_ref.shape[-1]):
+        lanes[part] = in_ref[0, :, column]
+    return [
+        jnp.concatenate(
+            [
+                lanes[part, pl.ds(parity, HALF, stride=2), :]
+                for part, _ in columns(in_ref.shape[-1])
+            ],
+            -1,
+        )
+        for parity in range(2)
+    ]
+
+
+def write_unsorted(out_ref, lanes, found):
+    for part, column in columns(out_ref.shape[-1]):
+        for parity in range(2):
+            lanes[part, pl.ds(parity, HALF, stride=2), :] = found[parity][:, column]
+        out_ref[0, :, column] = lanes[part]
+
+
+def lanes_of(width):
+    return [pltpu.VMEM((width // 128, TOK, 128), jnp.float32)]
+
+
+def norm_kernel(swap_ref, in_ref, gain_ref, bias_ref, sorted_ref, out_ref, lanes):
+    for parity, values in enumerate(read_sorted(in_ref, lanes)):
+        rows = pl.ds(parity * HALF, HALF)
+        sorted_ref[0, rows, :] = values
+        out_ref[0, rows, :] = layer_norm(values, gain_ref[...], bias_ref[...]).astype(jnp.bfloat16)
+
+
+def first_norm(swap, inputs, gain, bias):
+    width = inputs.shape[-1]
+    block = (1, TOK, width)
+    vector = pl.BlockSpec((1, width), lambda slot, swap: (0, 0))
+    own = pl.BlockSpec(block, lambda slot, swap: (slot, 0, 0))
+    return pl.pallas_call(
+        norm_kernel,
+        grid_spec=pltpu.PrefetchScalarGridSpec(
+            num_scalar_prefetch=1,
+            grid=(2,),
+            in_specs=[
+                pl.BlockSpec(block, lambda slot, swap: (slot ^ swap[0], 0, 0)),
+                vector,
+                vector,
+            ],
+            out_specs=[own, own],
+            scratch_shapes=lanes_of(width),
+        ),
+        out_shape=[
+            jax.ShapeDtypeStruct(inputs.shape, jnp.float32),
+            jax.ShapeDtypeStruct(inputs.shape, jnp.bfloat16),
+        ],
+        name="first_norm",
+    )(swap, inputs, gain[None], bias[None])
+
+
+def sort_kernel(swap_ref, in_ref, out_ref, lanes):
+    for parity, values in enumerate(read_sorted(in_ref, lanes)):
+        out_ref[0, pl.ds(parity * HALF, HALF), :] = values
+
+
+def unsort_kernel(swap_ref, in_ref, out_ref, lanes):
+    found = [in_ref[0, pl.ds(parity * HALF, HALF), :] for parity in range(2)]
+    write_unsorted(out_ref, lanes, found)
+
+
+def moved(kernel, swap, array):
+    block = (1, TOK, array.shape[-1])
+    return pl.pallas_call(
+        kernel,
+        grid_spec=pltpu.PrefetchScalarGridSpec(
+            num_scalar_prefetch=1,
+            grid=(2,),
+            in_specs=[pl.BlockSpec(block, lambda slot, swap: (slot ^ swap[0], 0, 0))],
+            out_specs=pl.BlockSpec(block, lambda slot, swap: (slot, 0, 0)),
+            scratch_shapes=lanes_of(block[-1]),
+        ),
+        out_shape=jax.ShapeDtypeStruct(array.shape, array.dtype),
+        name=kernel.__name__,
+    )(swap, array)
+
+
+def norm_back(values, grads, gain):
+    center = values - jnp.mean(values, axis=-1, keepdims=True)
+    scale = lax.rsqrt(jnp.mean(center * center, axis=-1, keepdims=True) + EPS)
+    unit = center * scale
+    scaled = grads * gain
+    mean_scaled = jnp.mean(scaled, axis=-1, keepdims=True)
+    mean_both = jnp.mean(scaled * unit, axis=-1, keepdims=True)
+    return scale * (scaled - mean_scaled - unit * mean_both)
+
+
+def last_kernel(swap_ref, values_ref, grads_ref, through_ref, gain_ref, out_ref, lanes):
+    found = []
+    for parity in range(2):
+        rows = pl.ds(parity * HALF, HALF)
+        grads = grads_ref[0, rows, :].astype(jnp.float32)
+        part = norm_back(values_ref[0, rows, :], grads, gain_ref[...])
+        found.append(through_ref[0, rows, :] + part)
+    write_unsorted(out_ref, lanes, found)
+
+
+def last_norm(swap, values, grads, through, gain):
+    width = values.shape[-1]
+    block = (1, TOK, width)
+    own = pl.BlockSpec(block, lambda slot, swap: (slot ^ swap[0], 0, 0))
+    return pl.pallas_call(
+        last_kernel,
+        grid_spec=pltpu.PrefetchScalarGridSpec(
+            num_scalar_prefetch=1,
+            grid=(2,),
+            in_specs=[own, own, own, pl.BlockSpec((1, width), lambda slot, swap: (0, 0))],
+            out_specs=pl.BlockSpec(block, lambda slot, swap: (slot, 0, 0)),
+            scratch_shapes=lanes_of(block[-1]),
+        ),
+        out_shape=jax.ShapeDtypeStruct(values.shape, jnp.float32),
+        name="last_norm",
+    )(swap, values, grads, through, gain[None])
+
+
+NT = (((1,), (1,)), ((), ()))
+NN = (((1,), (0,)), ((), ()))
+
+
+def dot(left, right, dims):
+    return lax.dot_general(left, right, dims, preferred_element_type=jnp.float32)
+
+
+def pieces():
+    for block in range(BLOCKS):
+        for parity in range(2):
+            place = block // 4 * SEG + parity * PAR + block % 4 * HALF
+            yield block, parity, place
+
+
+def load_row(place, parity_of_head, triple_ref, query_mark, key_mark, far_mark, query, far, key):
+    for block, parity, start in pieces():
+        rows = pl.ds(parity * HALF, HALF)
+        delta = place ^ block
+        query[pl.ds(start, HALF), :] = (
+            triple_ref[delta, rows, 0:128] + query_mark[0, pl.ds(start, HALF), :]
+        )
+        key[pl.ds(start, HALF), :] = (
+            triple_ref[delta, rows, 128:256] + key_mark[0, pl.ds(start, HALF), :]
+        )
+    for block in range(4):
+        rows = pl.ds(pl.multiple_of(parity_of_head * HALF, HALF), HALF)
+        far[pl.ds(block * HALF, HALF), :] = (
+            triple_ref[place ^ (block + 4), rows, 0:128]
+            + far_mark[0, pl.ds(block * HALF, HALF), :]
+        )
+
+
+def causal(parts, later):
+    keys = lax.broadcasted_iota(jnp.int32, parts.shape, 0)
+    queries = lax.broadcasted_iota(jnp.int32, parts.shape, 1)
+    return jnp.where(keys <= queries + later, parts, NEG)
+
+
+def aligned(start):
+    return pl.multiple_of(start, TILE)
+
+
+def groups(index):
+    segment, query_parity, key_parity = index >> 2, index >> 1 & 1, index & 1
+    query_base = segment * SEG + query_parity * PAR
+    key_base = segment * SEG + key_parity * PAR
+    later = jnp.where(query_parity < key_parity, -1, 0)
+    return query_base, key_base, later
+
+
+def forward_kernel(
+    info, triple_ref, query_mark, key_mark, far_mark, send_ref, result_ref, total_ref,
+    query, far, key, value, value_t, most, acc,
+):
+    head = pl.program_id(0)
+    place = info[0]
+    parity_of_head = (info[1] + head) & 1
+    load_row(
+        place, parity_of_head, triple_ref, query_mark, key_mark, far_mark, query, far, key
+    )
+    ones = jnp.where(lax.broadcasted_iota(jnp.int32, (HALF, 128), 1) == HEAD_DIM, 1.0, 0.0)
+    for block, parity, start in pieces():
+        rows = pl.ds(parity * HALF, HALF)
+        value[pl.ds(start, HALF), :] = (
+            triple_ref[place ^ block, rows, 256:384].astype(jnp.float32) + ones
+        )
+    for tile in range(LEN // TILE):
+        cols = pl.ds(tile * TILE, TILE)
+        value_t[:, cols] = value[cols, :].T.astype(jnp.bfloat16)
+    most[...] = jnp.full(most.shape, NEG, jnp.float32)
+    acc[...] = jnp.zeros(acc.shape, jnp.float32)
+
+    def update(column, parts):
+        cols = pl.ds(column, TILE)
+        old = most[0:1, cols]
+        new = old
+        for scores, _, _ in parts:
+            new = jnp.maximum(new, jnp.max(scores, axis=0, keepdims=True))
+        total = acc[:, cols] * jnp.exp2(old - new)
+        for scores, start, count in parts:
+            prob = jnp.exp2(scores - new).astype(jnp.bfloat16)
+            total = total + dot(value_t[0:80, pl.ds(start, count)], prob, NN)
+        acc[:, cols] = total
+        most[0:1, cols] = new
+
+    def near(index, carry):
+        query_base, key_base, later = groups(index)
+        for tile in range(TILES):
+            column = aligned(query_base + tile * TILE)
+            queries = query[pl.ds(column, TILE), :]
+            parts = []
+            if tile:
+                start = aligned(key_base)
+                scores = dot(key[pl.ds(start, tile * TILE), :], queries, NT)
+                parts.append((scores, start, tile * TILE))
+            start = aligned(key_base + tile * TILE)
+            scores = causal(dot(key[pl.ds(start, TILE), :], queries, NT), later)
+            parts.append((scores, start, TILE))
+            update(column, parts)
+        return carry
+
+    lax.fori_loop(0, 8, near, 0)
+    start = aligned(parity_of_head * PAR)
+    for tile in range(TILES):
+        queries = far[pl.ds(tile * TILE, TILE), :]
+        scores = dot(key[pl.ds(start, PAR), :], queries, NT)
+        update(aligned(SEG + parity_of_head * PAR + tile * TILE), [(scores, start, PAR)])
+
+    weight = acc[HEAD_DIM : HEAD_DIM + 1, :]
+    result = acc[0:HEAD_DIM, :] / weight
+    result_ref[0] = result
+    total_ref[0] = jnp.broadcast_to(most[0:1, :] + jnp.log2(weight), (8, LEN))
+    heads = pl.ds(pl.multiple_of(head * HEAD_DIM, HEAD_DIM), HEAD_DIM)
+    for block, parity, start in pieces():
+        send_ref[place ^ block, heads, parity * HALF : (parity + 1) * HALF] = result[
+            :, start : start + HALF
+        ].astype(jnp.bfloat16)
+
+
+def backward_kernel(
+    info, triple_ref, query_mark, key_mark, far_mark, grad_ref, result_ref, total_ref, out_ref,
+    query, far, key, value, key_t, grad_t, balance, query_grad, key_grad, value_grad, turned,
+):
+    head = pl.program_id(0)
+    place = info[0]
+    parity_of_head = (info[1] + head) & 1
+    load_row(
+        place, parity_of_head, triple_ref, query_mark, key_mark, far_mark, query, far, key
+    )
+    heads = pl.ds(pl.multiple_of(head * HEAD_DIM, HEAD_DIM), HEAD_DIM)
+    grad_t[HEAD_DIM:128, :] = jnp.zeros((128 - HEAD_DIM, LEN), jnp.bfloat16)
+    for block, parity, start in pieces():
+        rows = pl.ds(parity * HALF, HALF)
+        delta = place ^ block
+        value[pl.ds(start, HALF), :] = triple_ref[delta, rows, 256:384]
+        grad_t[0:HEAD_DIM, start : start + HALF] = grad_ref[
+            delta, heads, parity * HALF : (parity + 1) * HALF
+        ]
+    for tile in range(LEN // TILE):
+        cols = pl.ds(tile * TILE, TILE)
+        key_t[:, cols] = key[cols, :].astype(jnp.float32).T.astype(jnp.bfloat16)
+    balance[...] = jnp.sum(
+        grad_t[0:HEAD_DIM, :].astype(jnp.float32) * result_ref[0], axis=0, keepdims=True
+    )
+    query_grad[...] = jnp.zeros(query_grad.shape, jnp.float32)
+    key_grad[...] = jnp.zeros(key_grad.shape, jnp.float32)
+    value_grad[...] = jnp.zeros(value_grad.shape, jnp.float32)
+
+    def update(column, queries, start, count, later):
+        cols = pl.ds(column, TILE)
+        rows = pl.ds(start, count)
+        scores = dot(key[rows, :], queries, NT)
+        if later is not None:
+            scores = causal(scores, later)
+        prob = jnp.exp2(scores - total_ref[0, 0:1, cols])
+        grads = grad_t[:, cols]
+        flow = dot(value[rows, :], grads, NN)
+        slope = (prob * (flow - balance[0:1, cols])).astype(jnp.bfloat16)
+        value_grad[rows, :] += dot(prob.astype(jnp.bfloat16), grads, NT)
+        key_grad[rows, :] += dot(slope, queries, NN)
+        query_grad[0:HEAD_DIM, cols] += dot(key_t[0:HEAD_DIM, rows], slope, NN)
+
+    def near(index, carry):
+        query_base, key_base, later = groups(index)
+        for tile in range(TILES):
+            column = aligned(query_base + tile * TILE)
+            queries = query[pl.ds(column, TILE), :]
+            if tile:
+                update(column, queries, aligned(key_base), tile * TILE, None)
+            update(column, queries, aligned(key_base + tile * TILE), TILE, later)
+        return carry
+
+    lax.fori_loop(0, 8, near, 0)
+    start = aligned(parity_of_head * PAR)
+    for tile in range(TILES):
+        queries = far[pl.ds(tile * TILE, TILE), :]
+        column = aligned(SEG + parity_of_head * PAR + tile * TILE)
+        update(column, queries, start, PAR, None)
+
+    for tile in range(LEN // TILE):
+        cols = pl.ds(tile * TILE, TILE)
+        turned[cols, :] = query_grad[:, cols].T
+    first = lax.broadcasted_iota(jnp.int32, (HALF, 128), 1) < HEAD_DIM
+    for block, parity, start in pieces():
+        rows = pl.ds(parity * HALF, HALF)
+        delta = place ^ block
+        own = pl.ds(start, HALF)
+        pair = jnp.where(
+            first,
+            turned[own, :] * HEAD_DIM**-0.5,
+            pltpu.roll(key_grad[own, :], HEAD_DIM, axis=1) * (1 / LOG2E),
+        )
+        out_ref[delta, rows, 0:128] = pair.astype(jnp.bfloat16)
+        out_ref[delta, rows, 128:256] = jnp.where(first, value_grad[own, :], 0.0).astype(
+            jnp.bfloat16
+        )
+
+
+def whole(*shape):
+    return pl.BlockSpec(shape, lambda head, info: (0,) * len(shape))
+
+
+def per_head(*shape):
+    return pl.BlockSpec((1, *shape), lambda head, info: (head, *(0,) * len(shape)))
+
+
+def triple_spec():
+    return pl.BlockSpec((BLOCKS, TOK, 384), lambda head, info: (0, 0, head))
+
+
+def attention(info, triples, query_mark, key_mark, far_mark):
+    return pl.pallas_call(
+        forward_kernel,
+        grid_spec=pltpu.PrefetchScalarGridSpec(
+            num_scalar_prefetch=1,
+            grid=(OWN_HEADS,),
+            in_specs=[
+                triple_spec(),
+                per_head(LEN, 128),
+                per_head(LEN, 128),
+                per_head(PAR, 128),
+            ],
+            out_specs=[whole(BLOCKS, WIDTH, TOK), per_head(HEAD_DIM, LEN), per_head(8, LEN)],
+            scratch_shapes=[
+                pltpu.VMEM((LEN, 128), jnp.bfloat16),
+                pltpu.VMEM((PAR, 128), jnp.bfloat16),
+                pltpu.VMEM((LEN, 128), jnp.bfloat16),
+                pltpu.VMEM((LEN, 128), jnp.float32),
+                pltpu.VMEM((128, LEN), jnp.bfloat16),
+                pltpu.VMEM((8, LEN), jnp.float32),
+                pltpu.VMEM((80, LEN), jnp.float32),
+            ],
+        ),
+        out_shape=[
+            jax.ShapeDtypeStruct((BLOCKS, WIDTH, TOK), jnp.bfloat16),
+            jax.ShapeDtypeStruct((OWN_HEADS, HEAD_DIM, LEN), jnp.float32),
+            jax.ShapeDtypeStruct((OWN_HEADS, 8, LEN), jnp.float32),
+        ],
+        compiler_params=pltpu.CompilerParams(vmem_limit_bytes=VMEM_LIMIT),
+        name="attention",
+    )(info, triples, query_mark, key_mark, far_mark)
+
+
+def attention_back(info, triples, query_mark, key_mark, far_mark, grads, result, total):
+    return pl.pallas_call(
+        backward_kernel,
+        grid_spec=pltpu.PrefetchScalarGridSpec(
+            num_scalar_prefetch=1,
+            grid=(OWN_HEADS,),
+            in_specs=[
+                triple_spec(),
+                per_head(LEN, 128),
+                per_head(LEN, 128),
+                per_head(PAR, 128),
+                whole(BLOCKS, WIDTH, TOK),
+                per_head(HEAD_DIM, LEN),
+                per_head(8, LEN),
+            ],
+            out_specs=pl.BlockSpec((BLOCKS, TOK, 256), lambda head, info: (0, 0, head)),
+            scratch_shapes=[
+                pltpu.VMEM((LEN, 128), jnp.bfloat16),
+                pltpu.VMEM((PAR, 128), jnp.bfloat16),
+                pltpu.VMEM((LEN, 128), jnp.bfloat16),
+                pltpu.VMEM((LEN, 128), jnp.bfloat16),
+                pltpu.VMEM((128, LEN), jnp.bfloat16),
+                pltpu.VMEM((128, LEN), jnp.bfloat16),
+                pltpu.VMEM((1, LEN), jnp.float32),
+                pltpu.VMEM((128, LEN), jnp.float32),
+                pltpu.VMEM((LEN, 128), jnp.float32),
+                pltpu.VMEM((LEN, 128), jnp.float32),
+                pltpu.VMEM((LEN, 128), jnp.float32),
+            ],
+        ),
+        out_shape=jax.ShapeDtypeStruct((BLOCKS, TOK, OWN_HEADS * 256), jnp.bfloat16),
+        compiler_params=pltpu.CompilerParams(vmem_limit_bytes=VMEM_LIMIT),
+        name="attention_back",
+    )(info, triples, query_mark, key_mark, far_mark, grads, result, total)
+
+
+def marks(first_head, first_doc, padding):
+    heads = first_head + jnp.arange(OWN_HEADS, dtype=jnp.int32)[:, None, None]
+    column = jnp.arange(128, dtype=jnp.int32)[None, None, :] - HEAD_DIM
+
+    def members(place, dilation):
+        return (place - heads) % dilation == 0
+
+    def kind(place):
+        fifth, fourth, third, second = (
+            members(place, dilation)
+            for dilation in (FIFTH_DILATION, FOURTH_DILATION, THIRD_DILATION, SECOND_DILATION)
+        )
+        found = jnp.where(fifth, 0, jnp.where(fourth, 1, jnp.where(third, 2, 3)))
+        return jnp.where(second, found, 4)
+
+    def document(place):
+        return jnp.where(place < first_doc, 0, jnp.where(place >= LEN - padding, 2, 1))
+
+    index = jnp.arange(LEN, dtype=jnp.int32)
+    place = (index // SEG * SEG + index % PAR * 2 + index // PAR % 2)[None, :, None]
+    own, doc = kind(place), document(place)
+    query = (
+        ((column >= 0) & (column < 4) & (own == column))
+        | ((column >= 4) & (column < 8) & (own == column - 4))
+        | ((column >= 8) & (column < 11) & (doc == column - 8))
+    ).astype(jnp.bfloat16)
+
+    far_place = SEG + 2 * jnp.arange(PAR, dtype=jnp.int32)[None, :, None] + heads % 2
+    far_own, far_doc = kind(far_place), document(far_place)
+    far = (
+        ((column >= 8) & (column < 11) & (far_doc == column - 8))
+        | ((column >= 12) & (column < 16) & (far_own == column - 12))
+    ).astype(jnp.bfloat16)
+
+    row = column & 3
+    count = (
+        2
+        + ((row % 2 == 0) & (own % 2 == 0)).astype(jnp.int32)
+        + ((row < 2) & (own < 2)).astype(jnp.int32)
+        + ((row == 0) & (own == 0)).astype(jnp.int32)
+    )
+
+    def rounded(value):
+        return round(value * 64) / 64
+
+    log3, log5 = math.log2(3), math.log2(5)
+    high = jnp.where(count == 2, 1.0, jnp.where(count == 3, rounded(log3), rounded(log5)))
+    low = jnp.where(
+        count == 2,
+        0.0,
+        jnp.where(count == 3, log3 - rounded(log3), log5 - rounded(log5)),
+    )
+    across = jnp.where(count == 2, 0.0, jnp.where(count == 3, 1.0, 2.0))
+    even = own < 4
+    key = jnp.where((column >= 0) & (column < 4) & even, high, 0.0)
+    key = jnp.where((column >= 4) & (column < 8) & even, low, key)
+    key = jnp.where((column >= 8) & (column < 11) & (doc != column - 8), FAR, key)
+    key = jnp.where((column >= 12) & (column < 16) & even, across, key)
+    return query, key.astype(jnp.bfloat16), far
+
+
+def flipped(array, axis, bit):
+    zero, one = (lax.index_in_dim(array, i, axis, keepdims=False) for i in range(2))
+    return jnp.stack((pick(bit, zero, one), pick(bit, one, zero)), axis)
+
+
+def summed(array, core, x, y, z):
+    def add(parts, pairs):
+        keep, away = parts
+        return (keep.astype(jnp.float32) + send(away, pairs).astype(jnp.float32)).astype(
+            jnp.bfloat16
+        )
+
+    array = add(halves(array, core, 1), SWAP_CORE)
+    array = add(halves(array, x, 1), SWAP_X)
+    count, width = array.shape[1:]
+    array = add(halves(array.reshape(2, 2, 2, count, width), y, 2), SWAP_Y)
+    array = add(halves(array, z >> 1, 0), SWAP_Z_HIGH)
+    array = add(halves(array, z & 1, 1), SWAP_Z_LOW)
+    array = array.reshape(count, width)
+    array = joined(array, send(array, SWAP_X), x)
+    return joined(array, send(array, SWAP_CORE), core)
+
+
+def summed_heads(array, core, x, y, z):
+    def add(parts, pairs):
+        keep, away = parts
+        return (keep.astype(jnp.float32) + send(away, pairs).astype(jnp.float32)).astype(
+            jnp.bfloat16
+        )
+
+    array = add(halves(array, x, 1), SWAP_X)
+    count, width = array.shape[1:]
+    array = array.reshape(2, 2, 2, count, width)
+    array = add(halves(array, z >> 1, 0), SWAP_Z_HIGH)
+    array = add(halves(array, z & 1, 1), SWAP_Z_LOW)
+    keep, away = halves(array.reshape(2, count, width), y)
+    array = joined(keep, send(away, SWAP_Y), y)
+    array = jnp.stack((array, send(array, SWAP_CORE)), 1)
+    array = flipped(array, 1, core)
+    return joined(array, send(array, SWAP_X), x, 2)
+
+
+def packed_rows(
+    layer_input, doc_ids, cotangent, attn_norm_gain, attn_norm_bias, query_weight, query_bias,
+    key_weight, value_weight, value_bias, output_weight, output_bias, feed_norm_gain,
+    feed_norm_bias, up_weight, up_bias, down_weight, down_bias,
+):
+    bf16, f32 = jnp.bfloat16, jnp.float32
+    model = layer_input.shape[-1]
+    hidden_width = up_weight.shape[-1]
+    row, seq = lax.axis_index("row"), lax.axis_index("seq")
+    x, core, z, y = row >> 1, row & 1, seq >> 1, seq & 1
+    swap = (z & 1)[None].astype(jnp.int32)
+    place = 4 * core + 2 * (z & 1) + y
+    group = 2 * y + core
+    info = jnp.stack((place, OWN_HEADS * group)).astype(jnp.int32)
+
+    ordered, first = first_norm(swap, layer_input, attn_norm_gain, attn_norm_bias)
+
+    held = []
+    for slot in range(2):
+        block = send(first[slot], to_row(slot))
+        held.extend((block, send(block, SWAP_Y)))
+    held.extend([send(block, SWAP_CORE) for block in held])
+    normed = jnp.stack(held)
+
+    counts = jnp.stack((jnp.sum(doc_ids == 0, axis=1), jnp.sum(doc_ids < 0, axis=1)), 1)
+    counts = lax.all_gather(counts.astype(jnp.int32).reshape(1, 4), BOTH, tiled=True)
+    counts = jnp.sum(counts.reshape(4, 8, 2, 2), axis=1).reshape(2, 4, 2)
+    counts = lax.dynamic_index_in_dim(counts, x, 0, keepdims=False)
+    counts = lax.dynamic_index_in_dim(counts, z, 0, keepdims=False)
+    query_mark, key_mark, far_mark = marks(OWN_HEADS * group, counts[0], counts[1])
+
+    def own_columns(weight):
+        own = lax.dynamic_slice_in_dim(weight, group * WIDTH, WIDTH, weight.ndim - 1)
+        return own.reshape(*weight.shape[:-1], OWN_HEADS, HEAD_DIM)
+
+    query_own, key_own, value_own = map(own_columns, (query_weight, key_weight, value_weight))
+    triple_weight = jnp.stack((query_own, key_own, value_own), 2)
+    triple_weight = jnp.pad(triple_weight, ((0, 0),) * 3 + ((0, 128 - HEAD_DIM),))
+    triple_weight = triple_weight.reshape(model, OWN_HEADS * 384)
+    query_row, value_row = own_columns(query_bias), own_columns(value_bias)
+    triple_bias = jnp.stack((query_row, jnp.zeros_like(query_row), value_row), 1)
+    triple_bias = jnp.pad(triple_bias, ((0, 0), (0, 0), (0, 128 - HEAD_DIM))).reshape(-1)
+    scale = jnp.where(jnp.arange(OWN_HEADS * 384) % 384 < 128, LOG2E * HEAD_DIM**-0.5, 1.0)
+    triples = jnp.einsum("btd,df->btf", normed, triple_weight, preferred_element_type=f32)
+    triples = ((triples + triple_bias) * scale).astype(bf16)
+
+    sends, result, total = attention(info, triples, query_mark, key_mark, far_mark)
+    slabs = [send(sends[delta], to_owner(delta)) for delta in range(8)]
+    attended = jnp.stack(
+        [
+            jnp.concatenate([slabs[4 * high + 2 * slot + side] for side in (0, 1) for high in (0, 1)])
+            for slot in range(2)
+        ]
+    )
+
+    def other_order(array):
+        array = array.reshape(2, 2, WIDTH, model)
+        return flipped(flipped(array, 0, y), 1, z >> 1).reshape(4 * WIDTH, model)
+
+    output_own = other_order(output_weight)
+    docs = doc_ids.reshape(2, HALF, 2).transpose(0, 2, 1).reshape(2, TOK)
+    docs = flipped(docs, 0, z & 1)
+    masked_grad = jnp.where((docs >= 0)[..., None], moved(sort_kernel, swap, cotangent), 0.0)
+    down_grad = masked_grad.astype(bf16)
+    active_grad = project_back(down_grad, down_weight)
+
+    middle = ordered + output_bias
+    middle = middle + jnp.einsum("nft,fd->ntd", attended, output_own, preferred_element_type=f32)
+    second = layer_norm(middle, feed_norm_gain, feed_norm_bias).astype(bf16)
+    hidden = project(second, up_weight) + up_bias
+    active_full, gelu_pull = jax.vjp(jax.nn.gelu, hidden)
+    active = active_full.astype(bf16)
+    hidden_grad = gelu_pull(active_grad)[0].astype(bf16)
+    middle_part = norm_back(middle, project_back(hidden_grad, up_weight), feed_norm_gain)
+    middle_grad = masked_grad + middle_part
+    branch_grad = middle_grad.astype(bf16)
+    attended_grad = jnp.einsum("fd,ntd->nft", output_own, branch_grad, preferred_element_type=f32)
+    attended_grad = attended_grad.astype(bf16).reshape(2, 2, 2, WIDTH, TOK)
+    grads = jnp.stack(
+        [
+            send(attended_grad[delta >> 1 & 1, delta & 1, delta >> 2], inverse(to_owner(delta)))
+            for delta in range(8)
+        ]
+    )
+
+    out = moved(unsort_kernel, swap, middle + project(active, down_weight) + down_bias)
+    grad_down = weight_grad(active, down_grad)
+    grad_up = weight_grad(second, hidden_grad)
+    grad_output = jnp.einsum("nft,ntd->fd", attended, branch_grad, preferred_element_type=f32)
+    grad_output = other_order(grad_output)
+    early = jnp.concatenate(
+        (
+            grad_output.astype(bf16).reshape(8, -1, model),
+            grad_up.astype(bf16).reshape(8, -1, model),
+            grad_down.astype(bf16).reshape(8, -1, model),
+        ),
+        1,
+    )
+    early = summed(early, core, x, y, z).astype(f32)
+    output_rows = model // 8
+    up_rows = output_rows * hidden_width // model
+    grad_output = early[:output_rows]
+    grad_up = early[output_rows : output_rows + up_rows].reshape(model // 8, hidden_width)
+    grad_down = early[output_rows + up_rows :]
+
+    triple_grad = attention_back(
+        info, triples, query_mark, key_mark, far_mark, grads, result, total
+    )
+    back_weight = jnp.stack((query_own, key_own, value_own, jnp.zeros_like(key_own)), 2)
+    back_weight = back_weight.reshape(model, OWN_HEADS * 256)
+    first_grad = jnp.einsum("btf,df->btd", triple_grad, back_weight, preferred_element_type=f32)
+    far_half = send(first_grad[4:].astype(bf16), SWAP_CORE)
+    near_half = first_grad[:4] + far_half.astype(f32)
+    near_half = near_half.reshape(2, 2, TOK, model)
+    returned = []
+    for slot in range(2):
+        other = send(near_half[slot, 1].astype(bf16), SWAP_Y)
+        both = (near_half[slot, 0] + other.astype(f32)).astype(bf16)
+        returned.append(send(both, inverse(to_row(slot))))
+    input_grad = last_norm(swap, ordered, jnp.stack(returned), middle_grad, attn_norm_gain)
+
+    triple_sum = jnp.sum(triple_grad.astype(f32), axis=(0, 1)).reshape(OWN_HEADS, 4, HEAD_DIM)
+    triple_sum = triple_sum[:, :3].transpose(1, 0, 2).reshape(3, 1, WIDTH)
+    triple_sum = jnp.where(jnp.arange(4)[:, None] == group, triple_sum, 0.0).reshape(-1)
+    sums = jnp.concatenate(
+        (triple_sum, column_sum(branch_grad), column_sum(hidden_grad), column_sum(down_grad))
+    )
+    sums = lax.psum(sums, BOTH)
+    query_sum, key_sum, value_sum, output_sum, up_sum, down_sum = jnp.split(
+        sums, (model, 2 * model, 3 * model, 4 * model, 4 * model + hidden_width)
+    )
+
+    late = jnp.einsum("btd,btf->df", normed, triple_grad, preferred_element_type=f32)
+    late = late.reshape(model, OWN_HEADS, 4, HEAD_DIM)[:, :, :3].transpose(0, 2, 1, 3)
+    late = late.astype(bf16).reshape(8, model // 8, 3 * WIDTH)
+    late = summed_heads(late, core, x, y, z).astype(f32)
+    late = late.reshape(4, model // 8, 3, WIDTH).transpose(2, 1, 0, 3)
+    grad_query, grad_key, grad_value = late.reshape(3, model // 8, model)
+
+    def own_rows(array):
+        count = array.shape[0] // 8
+        return lax.dynamic_slice_in_dim(array, seq * count, count, 0)
+
+    def norm_grads(gain, bias, parts):
+        bias_grad = jnp.zeros((model // 8,), f32)
+        both = bias_grad
+        for weight, grad, total in parts:
+            mine = own_rows(weight).astype(f32)
+            bias_grad = bias_grad + jnp.sum(mine * total, axis=1)
+            both = both + jnp.sum(mine * grad, axis=1)
+        return (both - own_rows(bias) * bias_grad) / own_rows(gain), bias_grad
+
+    grad_feed_gain, grad_feed_bias = norm_grads(
+        feed_norm_gain, feed_norm_bias, ((up_weight, grad_up, up_sum),)
+    )
+    grad_attn_gain, grad_attn_bias = norm_grads(
+        attn_norm_gain,
+        attn_norm_bias,
+        (
+            (query_weight, grad_query, query_sum),
+            (key_weight, grad_key, key_sum),
+            (value_weight, grad_value, value_sum),
+        ),
+    )
+    return (
+        out,
+        input_grad,
+        grad_attn_gain,
+        grad_attn_bias,
+        grad_query,
+        own_rows(query_sum),
+        grad_key,
+        grad_value,
+        own_rows(value_sum),
+        grad_output,
+        own_rows(output_sum),
+        grad_feed_gain,
+        grad_feed_bias,
+        grad_up,
+        own_rows(up_sum),
+        grad_down,
+        own_rows(down_sum),
+    )
+
+
 def solution(mesh):
     placed = (
         P("row", "seq", None),
@@ -428,8 +1195,9 @@
         P(),
         P(),
     )
+    chosen = packed_rows if dict(mesh.shape) == {"row": 4, "seq": 8} else per_device
     return jax.shard_map(
-        per_device,
+        chosen,
         mesh=mesh,
         in_specs=placed,
         out_specs=(

time: 6100 us -> 685 us (0.11)
  local copies, waits for them, and re-layouts: 2990 us -> 60.3 us
  waiting for transfers between devices: 1020 us -> 137 us
  other arithmetic: 787 us -> 75.1 us
  matrix products: 651 us -> 78.6 us
  blocking collectives: 462 us -> 133 us
  loops' own time: 117 us -> 0 us
  Pallas kernels: 0 us -> 101 us
  starting transfers between devices: 5.92 us -> 86.1 us
    broadcast_in_dim x1656 -> x3, local copies, waits for them, and re-layouts: 848 us -> 2.62 us  [the longest x1 1.27 us: first_norm(): gain[None]]
    ppermute x6 -> x42, waiting for transfers between devices: 922 us -> 137 us  [send(): return lax.ppermute(array, BOTH, pairs)]
    dynamic_slice x769 -> x9, local copies, waits for them, and re-layouts: 586 us -> 7.34 us  [the longest x4 4.36 us: own_columns(): lax.dynamic_slice_in_dim(weight, group * WIDTH, WIDTH, weight.ndim - 1)]
    slice x129 -> x2, local copies, waits for them, and re-layouts: 560 us -> 2.37 us  [the longest x1 1.78 us: packed_rows(): far_half = send(first_grad[4:].astype(bf16), SWAP_CORE)]
    dot_general x421 -> x6, matrix products: 579 us -> 28.2 us  [the longest x1 8.49 us: packed_rows(): jnp.einsum('btd,df->btf', normed, triple_weight, preferred_element_type=f32)]
    all_gather x1, blocking collectives: 418 us -> 70.6 us  [packed_rows(): lax.all_gather(counts.astype(jnp.int32).reshape(1, 4), BOTH, tiled=True)]
    reshape x248 -> x7, local copies, waits for them, and re-layouts: 213 us -> 10.4 us  [the longest x1 8.46 us: packed_rows(): grad_up.astype(bf16).reshape(8, -1, model)]
    unnamed x245 -> x131, local copies, waits for them, and re-layouts: 197 us -> 20.3 us
where the time goes in v1:
time: 685 us; the launch traced here: 674 us
  waiting for transfers between devices  137 us (20%)
  blocking collectives  133 us (19%)
  Pallas kernels  101 us (15%)
  starting transfers between devices  86.1 us (13%)
  matrix products  78.6 us (11%)
  other arithmetic  75.1 us (11%)
  local copies, waits for them, and re-layouts  60.3 us (9%)
    ppermute x42, waiting for transfers between devices, send(): return lax.ppermute(array, BOTH, pairs)  137 us
    ppermute x42, starting transfers between devices, send(): return lax.ppermute(array, BOTH, pairs)  86.1 us
    all_gather x1, blocking collectives, packed_rows(): lax.all_gather(counts.astype(jnp.int32).reshape(1, 4), BOTH, tiled=True)  70.6 us
    psum x1, blocking collectives, packed_rows(): sums = lax.psum(sums, BOTH)  62.4 us
    pallas_call x1, Pallas kernels, attention_back(): pl.pallas_call(backward_kernel, grid_spec=pltpu.PrefetchScalarGridSpec(nu...  49.2 us
    pallas_call x1, Pallas kernels, attention(): pl.pallas_call(forward_kernel, grid_spec=pltpu.PrefetchScalarGridSpec(num...  37.9 us
    unnamed x131, local copies, waits for them, and re-layouts  20.3 us
    dot_general x2, matrix products, project(): jnp.einsum('ntd,df->ntf', inputs, weight, preferred_element_type=jnp.floa...  18.9 us
  transfers between devices with their start and end apart: 42, of which 18 were waited for; matrix products, arithmetic and copies ran while one was open for 16% of the time, Pallas kernels for 9%

profile of v1, /device:TPU:1, one launch (start us, length us, event | category | flops | bytes accessed | tf_op | source)
XLA Modules:
  0.0 673.7 jit_solution(8918603463980183876)
XLA Ops:
  8.6 5.6 collective-permute-start
  19.5 70.6 %all-gather = s32[32,1,4]{2,1,0:T(1,128)S(1)} all-gather(s32[1,1,4]{2,1,0:T(1,128)S(1)} %reshape.1056), channel_id=1, replica_groups=mesh['row'=4,'seq'=8] {'row','seq'}, dimensions={0}, use_global_device_ids=true | all-gather | bytes 528 | tf_op jit(solution)/shard_map/all_gather | solution.py:1017
  100.8 7.5 %select_convert_fusion.key_mark = bf16[3,3072,128]{2,1,0:T(8,128)(2,1)} fusion(pred[3072,128]{1,0:T(8,128)(4,1)S(1)} %get-tuple-element.99, pred[3,3072]{1,0:T(4,128)(4,1)S(1)} %get-tuple-element.102, pred[128]{0:T(512)(128)(4,1)S(1)} %get-tuple-element.125, pred[3,3072]{1,0:T(4,128)(4,1)S(1)} %get-tuple-element.104, ...), kind=kLoop, calls=%fused_computation.30 | loop fusion | flops 29491200 | bytes 2790144 | tf_op jit(solution)/shard_map/convert_element_type | solution.py:947
  121.2 6.7 %collective-permute-start.4 = (bf16[384,768]{1,0:T(8,128)(2,1)}, bf16[384,768]{1,0:T(8,128)(2,1)S(1)}, u32[]{:S(2)}, u32[]{:S(2)}) collective-permute-start(bf16[384,768]{1,0:T(8,128)(2,1)} %collective-permute-done), channel_id=1, source_target_pairs={{0,8},{1,9},{2,10},{3,11},{4,12},{5,13},{6,14},{7,15},{8,0},{9,1},... | collective-permute-start | bytes 1769480 | tf_op jit(solution)/shard_map/ppermute | solution.py:448
  128.0 5.7 collective-permute-start.5
  136.0 4.4 collective-permute-start.7
  144.2 8.5 %multiply_convert_fusion.triple_ref = bf16[8,384,1152]{2,1,0:T(8,128)(2,1)} fusion(bf16[8,384,768]{2,1,0:T(8,128)(2,1)S(1)} %bitcast_dynamic-update-slice_fusion, bf16[768,1152,1]{0,1,2:T(8,128)(2,1)S(1)} %bitcast.226, f32[1152]{0:T(1024)S(1)} %copy-done.35, f32[1152]{0:T(1024)S(1)} %add.521), kind=kOutput, calls=%fused_computation | convolution fusion | flops 5446434816 | bytes 13575168 | tf_op jit(solution)/shard_map/btd,df->btf/dot_general | solution.py:1035
  152.7 37.9 %attention.1 = (bf16[8,192,384]{2,1,0:T(8,128)(2,1)}, f32[3,64,3072]{2,1,0:T(8,128)}, f32[3,8,3072]{2,1,0:T(8,128)}) custom-call(s32[2]{0:T(128)} %pad_add_fusion.1.info, bf16[8,384,1152]{2,1,0:T(8,128)(2,1)} %multiply_convert_fusion.triple_ref, bf16[3,3072,128]{2,1,0:T(8,128)(2,1)} %or_convert_fusion.query_mark, ...), custom_call_target="tpu_custom_call" | custom-call | tf_op jit(solution)/shard_map/attention/pallas_call | solution.py:821
  206.6 5.5 collective-permute-start.8
  226.4 6.5 fusion.13
  233.0 12.1 %convert_reduce_fusion = (f32[3072]{0:T(1024)}, bf16[2,384,3072]{2,1,0:T(8,128)(2,1)S(1)}) fusion(f32[2,384,3072]{2,1,0:T(8,128)} %fusion.13, f32[3072]{0:T(1024)S(1)} %copy-done.39, bf16[2,384,768]{2,1,0:T(8,128)(2,1)S(1)} %copy-done.17, bf16[3072,768]{1,0:T(8,128)(2,1)S(1)} %bitcast.237), kind=kOutput, calls=%fused_computation.13 | convolution fusion | flops 3678139392 | bytes 20078592 | tf_op jit(solution)/shard_map/ntf,df->ntd/dot_general | solution.py:49
  245.1 5.5 multiply_reduce_fusion.2
  250.6 6.3 bitcast_convert_fusion.1
  257.0 7.6 %bitcast_convert_fusion = bf16[3072,768]{1,0:T(8,128)(2,1)} fusion(bf16[2,384,768]{2,1,0:T(8,128)(2,1)S(1)} %copy-done.17, f32[2,384,3072]{2,1,0:T(8,128)S(1)} %copy-done.43, f32[3072]{0:T(1024)S(1)} %copy-done.39), kind=kOutput, calls=%fused_computation.11 | convolution fusion | flops 3649830912 | bytes 15347712 | tf_op jit(solution)/shard_map/ntd,ntf->df/dot_general | solution.py:53
  264.5 8.5 %reshape.1050 = bf16[8,384,768]{2,1,0:T(8,128)(2,1)} reshape(bf16[768,3072]{1,0:T(8,128)(2,1)} %bitcast_convert_fusion.1) | data formatting | bytes 9437184 | tf_op jit(solution)/shard_map/reshape | solution.py:1085
  292.9 12.3 %add_add_fusion.in_ref = f32[2,384,768]{2,1,0:T(8,128)} fusion(f32[2,384,768]{2,1,0:T(8,128)S(1)} %copy-done.8, bf16[3072,768]{1,0:T(8,128)(2,1)} %param.34, f32[768]{0:T(1024)S(1)} %copy-done.42, f32[2,384,3072]{2,1,0:T(8,128)} %fusion.13, f32[3072]{0:T(1024)S(1)} %copy-done.40), kind=kOutput, calls=%fused_computation.43 | convolution fusion | flops 3648651264 | bytes 18889728 | tf_op jit(solution)/shard_map/ntd,df->ntf/dot_general | solution.py:45
  320.7 7.7 %collective-permute-start.23 = (bf16[192,384]{1,0:T(8,128)(2,1)S(1)}, bf16[192,384]{1,0:T(8,128)(2,1)S(1)}, u32[]{:S(2)}, u32[]{:S(2)}) collective-permute-start(bf16[192,384]{1,0:T(8,128)(2,1)S(1)} %get-tuple-element.62), channel_id=1, source_target_pairs={{0,11},{1,10},{2,9},{3,8},{4,3},{5,2},{6,1},{7,0},{8,15},{9,14},{1... | collective-permute-start | bytes 442376 | tf_op jit(solution)/shard_map/ppermute | solution.py:448
  333.0 49.2 %attention_back.1 = bf16[8,384,768]{2,1,0:T(8,128)(2,1)} custom-call(s32[2]{0:T(128)} %pad_add_fusion.1.info, bf16[8,384,1152]{2,1,0:T(8,128)(2,1)} %multiply_convert_fusion.triple_ref, bf16[3,3072,128]{2,1,0:T(8,128)(2,1)} %or_convert_fusion.query_mark, bf16[3,3072,128]{2,1,0:T(8,128)(2,1)} %select_convert_fusion.key_mark, ...), custom_call_target="tpu_custom_call" | custom-call | tf_op jit(solution)/shard_map/attention_back/pallas_call | solution.py:854
  382.2 7.8 %bitcast_convert_fusion.2 = bf16[768,768]{0,1:T(8,128)(2,1)S(1)} fusion(bf16[8,384,768]{2,1,0:T(8,128)(2,1)} %copy-done.27, bf16[8,384,768]{2,1,0:T(8,128)(2,1)} %attention_back.1), kind=kOutput, calls=%fused_computation.37 | convolution fusion | flops 3624468480 | bytes 10616832 | tf_op jit(solution)/shard_map/btd,btf->df/dot_general | solution.py:1124
  390.0 4.8 add_convert_fusion
  416.3 48.9 %collective-permute-done.29 = bf16[8,48,576]{2,1,0:T(8,128)(2,1)S(1)} collective-permute-done((bf16[8,48,576]{2,1,0:T(8,128)(2,1)S(1)}, bf16[8,48,576]{2,1,0:T(8,128)(2,1)S(1)}, u32[]{:S(2)}, u32[]{:S(2)}) %collective-permute-start.29) | collective-permute-done | bytes 442400 | tf_op jit(solution)/shard_map/ppermute | solution.py:448
  468.6 7.7 %collective-permute-start.30 = (bf16[1,2,2,48,576]{4,3,2,1,0:T(8,128)(2,1)S(1)}, bf16[1,2,2,48,576]{4,3,2,1,0:T(8,128)(2,1)S(1)}, u32[]{:S(2)}, u32[]{:S(2)}) collective-permute-start(bf16[1,2,2,48,576]{4,3,2,1,0:T(8,128)(2,1)S(1)} %copy.104), channel_id=1, source_target_pairs={{0,4},{1,5},{2,6},{3,7},{4,0},{5,1},{6,2},{7,3},{8,12},{9,13},{10,... | collective-permute-start | bytes 663560 | tf_op jit(solution)/shard_map/ppermute | solution.py:448
  477.3 9.8 %collective-permute-done.30 = bf16[1,2,2,48,576]{4,3,2,1,0:T(8,128)(2,1)S(1)} collective-permute-done((bf16[1,2,2,48,576]{4,3,2,1,0:T(8,128)(2,1)S(1)}, bf16[1,2,2,48,576]{4,3,2,1,0:T(8,128)(2,1)S(1)}, u32[]{:S(2)}, u32[]{:S(2)}) %collective-permute-start.30) | collective-permute-done | bytes 221216 | tf_op jit(solution)/shard_map/ppermute | solution.py:448
  487.3 4.3 add_convert_fusion.1
  494.4 62.4 %psum.7 = f32[6912]{0:T(1024)S(1)} all-reduce(f32[6912]{0:T(1024)S(1)} %pad_maximum_fusion.15), channel_id=1, replica_groups=mesh['row'=4,'seq'=8] {'row','seq'}, use_global_device_ids=true, to_apply=%region_14.15 | all-reduce | flops 6912 | bytes 55296 | tf_op jit(solution)/shard_map/psum | solution.py:1119
  576.0 21.8 %collective-permute-done.38 = bf16[1,2,1,216,768]{4,3,2,1,0:T(8,128)(2,1)S(1)} collective-permute-done((bf16[1,2,1,216,768]{4,3,2,1,0:T(8,128)(2,1)S(1)}, bf16[1,2,1,216,768]{4,3,2,1,0:T(8,128)(2,1)S(1)}, u32[]{:S(2)}, u32[]{:S(2)}) %collective-permute-start.38) | collective-permute-done | bytes 663584 | tf_op jit(solution)/shard_map/ppermute | solution.py:448
  601.3 5.1 collective-permute-done.39
  608.6 4.6 collective-permute-done.25
  614.0 11.9 %collective-permute-done.27 = bf16[384,768]{1,0:T(8,128)(2,1)} collective-permute-done((bf16[384,768]{1,0:T(8,128)(2,1)}, bf16[384,768]{1,0:T(8,128)(2,1)}, u32[]{:S(2)}, u32[]{:S(2)}) %collective-permute-start.27) | collective-permute-done | bytes 589856 | tf_op jit(solution)/shard_map/ppermute | solution.py:448
  641.9 4.4 collective-permute-done.28
  646.3 13.5 %collective-permute-done.26 = bf16[384,768]{1,0:T(8,128)(2,1)} collective-permute-done((bf16[384,768]{1,0:T(8,128)(2,1)S(1)}, bf16[384,768]{1,0:T(8,128)(2,1)}, u32[]{:S(2)}, u32[]{:S(2)}) %collective-permute-start.26) | collective-permute-done | bytes 589856 | tf_op jit(solution)/shard_map/ppermute | solution.py:448
  662.2 4.5 last_norm.1
  (355 shorter events, 190.9 us)
Async XLA Ops:
  8.6 102.9 %collective-permute-start = (bf16[384,768]{1,0:T(8,128)(2,1)S(1)}, bf16[384,768]{1,0:T(8,128)(2,1)}, u32[]{:S(2)}, u32[]{:S(2)}) collective-permute-start(bf16[384,768]{1,0:T(8,128)(2,1)S(1)} %get-tuple-element.79), channel_id=1, source_target_pairs={{0,0},{1,1},{2,2},{3,3},{4,8},{5,9},{6,10},{7,11},{8,4},{9,5},{10,... | collective-permute-start | bytes 1769480 | tf_op jit(solution)/shard_map/ppermute | solution.py:448
  14.2 104.5 %collective-permute-start.2 = (bf16[384,768]{1,0:T(8,128)(2,1)}, bf16[384,768]{1,0:T(8,128)(2,1)}, u32[]{:S(2)}, u32[]{:S(2)}) collective-permute-start(bf16[384,768]{1,0:T(8,128)(2,1)} %get-tuple-element.78), channel_id=1, source_target_pairs={{0,2},{1,3},{2,0},{3,1},{4,10},{5,11},{6,8},{7,9},{8,6},{9,7},{10,... | collective-permute-start | bytes 1769480 | tf_op jit(solution)/shard_map/ppermute | solution.py:448
  111.5 16.5 %collective-permute-start.1 = (bf16[384,768]{1,0:T(8,128)(2,1)}, bf16[384,768]{1,0:T(8,128)(2,1)}, u32[]{:S(2)}, u32[]{:S(2)}) collective-permute-start(bf16[384,768]{1,0:T(8,128)(2,1)} %collective-permute-done), channel_id=1, source_target_pairs={{0,1},{1,0},{2,3},{3,2},{4,5},{5,4},{6,7},{7,6},{8,9},{9,8},{10,11... | collective-permute-start | bytes 1769480 | tf_op jit(solution)/shard_map/ppermute | solution.py:448
  118.7 17.3 %collective-permute-start.3 = (bf16[384,768]{1,0:T(8,128)(2,1)}, bf16[384,768]{1,0:T(8,128)(2,1)S(1)}, u32[]{:S(2)}, u32[]{:S(2)}) collective-permute-start(bf16[384,768]{1,0:T(8,128)(2,1)} %collective-permute-done.2), channel_id=1, source_target_pairs={{0,1},{1,0},{2,3},{3,2},{4,5},{5,4},{6,7},{7,6},{8,9},{9,8},{10,11... | collective-permute-start | bytes 1769480 | tf_op jit(solution)/shard_map/ppermute | solution.py:448
  121.2 19.3 %collective-permute-start.4 = (bf16[384,768]{1,0:T(8,128)(2,1)}, bf16[384,768]{1,0:T(8,128)(2,1)S(1)}, u32[]{:S(2)}, u32[]{:S(2)}) collective-permute-start(bf16[384,768]{1,0:T(8,128)(2,1)} %collective-permute-done), channel_id=1, source_target_pairs={{0,8},{1,9},{2,10},{3,11},{4,12},{5,13},{6,14},{7,15},{8,0},{9,1},... | collective-permute-start | bytes 1769480 | tf_op jit(solution)/shard_map/ppermute | solution.py:448
  128.0 12.6 %collective-permute-start.6 = (bf16[384,768]{1,0:T(8,128)(2,1)}, bf16[384,768]{1,0:T(8,128)(2,1)S(1)}, u32[]{:S(2)}, u32[]{:S(2)}) collective-permute-start(bf16[384,768]{1,0:T(8,128)(2,1)} %collective-permute-done.2), channel_id=1, source_target_pairs={{0,8},{1,9},{2,10},{3,11},{4,12},{5,13},{6,14},{7,15},{8,0},{9,1},... | collective-permute-start | bytes 1769480 | tf_op jit(solution)/shard_map/ppermute | solution.py:448
  128.0 12.5 %collective-permute-start.5 = (bf16[384,768]{1,0:T(8,128)(2,1)}, bf16[384,768]{1,0:T(8,128)(2,1)S(1)}, u32[]{:S(2)}, u32[]{:S(2)}) collective-permute-start(bf16[384,768]{1,0:T(8,128)(2,1)} %collective-permute-done.1), channel_id=1, source_target_pairs={{0,8},{1,9},{2,10},{3,11},{4,12},{5,13},{6,14},{7,15},{8,0},{9,1},... | collective-permute-start | bytes 1769480 | tf_op jit(solution)/shard_map/ppermute | solution.py:448
  193.0 11.2 %collective-permute-start.14 = (bf16[192,384]{1,0:T(8,128)(2,1)}, bf16[192,384]{1,0:T(8,128)(2,1)}, u32[]{:S(2)}, u32[]{:S(2)}) collective-permute-start(bf16[192,384]{1,0:T(8,128)(2,1)} %get-tuple-element.72), channel_id=1, source_target_pairs={{0,3},{1,2},{2,1},{3,0},{4,11},{5,10},{6,9},{7,8},{8,7},{9,6},{10,... | collective-permute-start | bytes 442376 | tf_op jit(solution)/shard_map/ppermute | solution.py:448
  194.6 12.0 %collective-permute-start.13 = (bf16[192,384]{1,0:T(8,128)(2,1)}, bf16[192,384]{1,0:T(8,128)(2,1)}, u32[]{:S(2)}, u32[]{:S(2)}) collective-permute-start(bf16[192,384]{1,0:T(8,128)(2,1)} %get-tuple-element.73), channel_id=1, source_target_pairs={{0,6},{1,7},{2,4},{3,5},{4,14},{5,15},{6,12},{7,13},{8,2},{9,3},{1... | collective-permute-start | bytes 442376 | tf_op jit(solution)/shard_map/ppermute | solution.py:448
  197.7 15.7 %collective-permute-start.12 = (bf16[192,384]{1,0:T(8,128)(2,1)}, bf16[192,384]{1,0:T(8,128)(2,1)}, u32[]{:S(2)}, u32[]{:S(2)}) collective-permute-start(bf16[192,384]{1,0:T(8,128)(2,1)} %get-tuple-element.74), channel_id=1, source_target_pairs={{0,2},{1,3},{2,0},{3,1},{4,10},{5,11},{6,8},{7,9},{8,6},{9,7},{10,... | collective-permute-start | bytes 442376 | tf_op jit(solution)/shard_map/ppermute | solution.py:448
  201.1 16.5 %collective-permute-start.11 = (bf16[192,384]{1,0:T(8,128)(2,1)}, bf16[192,384]{1,0:T(8,128)(2,1)}, u32[]{:S(2)}, u32[]{:S(2)}) collective-permute-start(bf16[192,384]{1,0:T(8,128)(2,1)} %get-tuple-element.75), channel_id=1, source_target_pairs={{0,5},{1,4},{2,7},{3,6},{4,13},{5,12},{6,15},{7,14},{8,1},{9,0},{1... | collective-permute-start | bytes 442376 | tf_op jit(solution)/shard_map/ppermute | solution.py:448
  201.2 18.5 %collective-permute-start.10 = (bf16[192,384]{1,0:T(8,128)(2,1)}, bf16[192,384]{1,0:T(8,128)(2,1)}, u32[]{:S(2)}, u32[]{:S(2)}) collective-permute-start(bf16[192,384]{1,0:T(8,128)(2,1)} %get-tuple-element.76), channel_id=1, source_target_pairs={{0,1},{1,0},{2,3},{3,2},{4,9},{5,8},{6,11},{7,10},{8,5},{9,4},{10,... | collective-permute-start | bytes 442376 | tf_op jit(solution)/shard_map/ppermute | solution.py:448
  204.2 15.8 %collective-permute-start.9 = (bf16[192,384]{1,0:T(8,128)(2,1)S(1)}, bf16[192,384]{1,0:T(8,128)(2,1)}, u32[]{:S(2)}, u32[]{:S(2)}) collective-permute-start(bf16[192,384]{1,0:T(8,128)(2,1)S(1)} %get-tuple-element.77), channel_id=1, source_target_pairs={{0,4},{1,5},{2,6},{3,7},{4,12},{5,13},{6,14},{7,15},{8,0},{9,1},{1... | collective-permute-start | bytes 442376 | tf_op jit(solution)/shard_map/ppermute | solution.py:448
  206.6 14.9 %collective-permute-start.8 = (bf16[192,384]{1,0:T(8,128)(2,1)S(1)}, bf16[192,384]{1,0:T(8,128)(2,1)}, u32[]{:S(2)}, u32[]{:S(2)}) collective-permute-start(bf16[192,384]{1,0:T(8,128)(2,1)S(1)} %get-tuple-element.70), channel_id=1, source_target_pairs={{0,0},{1,1},{2,2},{3,3},{4,8},{5,9},{6,10},{7,11},{8,4},{9,5},{10,... | collective-permute-start | bytes 442376 | tf_op jit(solution)/shard_map/ppermute | solution.py:448
  283.0 107.0 %collective-permute-start.35 = (bf16[8,432,768]{2,1,0:T(8,128)(2,1)}, bf16[8,432,768]{2,1,0:T(8,128)(2,1)}, u32[]{:S(2)}, u32[]{:S(2)}) collective-permute-start(bf16[8,432,768]{2,1,0:T(8,128)(2,1)} %broadcast_select_fusion), channel_id=1, source_target_pairs={{0,8},{1,9},{2,10},{3,11},{4,12},{5,13},{6,14},{7,15},{8,0},{9,1},... | collective-permute-start | bytes 15925256 | tf_op jit(solution)/shard_map/ppermute | solution.py:448
  291.0 24.2 %collective-permute-start.16 = (bf16[192,384]{1,0:T(8,128)(2,1)}, bf16[192,384]{1,0:T(8,128)(2,1)S(1)}, u32[]{:S(2)}, u32[]{:S(2)}) collective-permute-start(bf16[192,384]{1,0:T(8,128)(2,1)} %get-tuple-element.69), channel_id=1, source_target_pairs={{0,0},{1,1},{2,2},{3,3},{4,8},{5,9},{6,10},{7,11},{8,4},{9,5},{10,... | collective-permute-start | bytes 442376 | tf_op jit(solution)/shard_map/ppermute | solution.py:448
  315.9 12.6 %collective-permute-start.20 = (bf16[192,384]{1,0:T(8,128)(2,1)S(1)}, bf16[192,384]{1,0:T(8,128)(2,1)S(1)}, u32[]{:S(2)}, u32[]{:S(2)}) collective-permute-start(bf16[192,384]{1,0:T(8,128)(2,1)S(1)} %get-tuple-element.65), channel_id=1, source_target_pairs={{0,8},{1,9},{2,10},{3,11},{4,0},{5,1},{6,2},{7,3},{8,12},{9,13},{1... | collective-permute-start | bytes 442376 | tf_op jit(solution)/shard_map/ppermute | solution.py:448
  316.8 11.7 %collective-permute-start.21 = (bf16[192,384]{1,0:T(8,128)(2,1)S(1)}, bf16[192,384]{1,0:T(8,128)(2,1)S(1)}, u32[]{:S(2)}, u32[]{:S(2)}) collective-permute-start(bf16[192,384]{1,0:T(8,128)(2,1)S(1)} %get-tuple-element.64), channel_id=1, source_target_pairs={{0,9},{1,8},{2,11},{3,10},{4,1},{5,0},{6,3},{7,2},{8,13},{9,12},{1... | collective-permute-start | bytes 442376 | tf_op jit(solution)/shard_map/ppermute | solution.py:448
  320.7 11.2 %collective-permute-start.23 = (bf16[192,384]{1,0:T(8,128)(2,1)S(1)}, bf16[192,384]{1,0:T(8,128)(2,1)S(1)}, u32[]{:S(2)}, u32[]{:S(2)}) collective-permute-start(bf16[192,384]{1,0:T(8,128)(2,1)S(1)} %get-tuple-element.62), channel_id=1, source_target_pairs={{0,11},{1,10},{2,9},{3,8},{4,3},{5,2},{6,1},{7,0},{8,15},{9,14},{1... | collective-permute-start | bytes 442376 | tf_op jit(solution)/shard_map/ppermute | solution.py:448
  398.8 88.4 %collective-permute-start.36 = (bf16[8,216,768]{2,1,0:T(8,128)(2,1)}, bf16[8,216,768]{2,1,0:T(8,128)(2,1)}, u32[]{:S(2)}, u32[]{:S(2)}) collective-permute-start(bf16[8,216,768]{2,1,0:T(8,128)(2,1)} %broadcast_select_fusion.1), channel_id=1, source_target_pairs={{0,16},{1,17},{2,18},{3,19},{4,20},{5,21},{6,22},{7,23},{8,24},{9,... | collective-permute-start | bytes 7962632 | tf_op jit(solution)/shard_map/ppermute | solution.py:448
  406.0 164.2 %collective-permute-start.24 = (bf16[4,384,768]{2,1,0:T(8,128)(2,1)}, bf16[4,384,768]{2,1,0:T(8,128)(2,1)}, u32[]{:S(2)}, u32[]{:S(2)}) collective-permute-start(bf16[4,384,768]{2,1,0:T(8,128)(2,1)} %slice.282), channel_id=1, source_target_pairs={{0,8},{1,9},{2,10},{3,11},{4,12},{5,13},{6,14},{7,15},{8,0},{9,1},... | collective-permute-start | bytes 7077896 | tf_op jit(solution)/shard_map/ppermute | solution.py:448
  412.3 52.9 %collective-permute-start.29 = (bf16[8,48,576]{2,1,0:T(8,128)(2,1)S(1)}, bf16[8,48,576]{2,1,0:T(8,128)(2,1)S(1)}, u32[]{:S(2)}, u32[]{:S(2)}) collective-permute-start(bf16[8,48,576]{2,1,0:T(8,128)(2,1)S(1)} %copy.102), channel_id=1, source_target_pairs={{0,16},{1,17},{2,18},{3,19},{4,20},{5,21},{6,22},{7,23},{8,24},{9,... | collective-permute-start | bytes 1327112 | tf_op jit(solution)/shard_map/ppermute | solution.py:448
  468.6 18.5 %collective-permute-start.30 = (bf16[1,2,2,48,576]{4,3,2,1,0:T(8,128)(2,1)S(1)}, bf16[1,2,2,48,576]{4,3,2,1,0:T(8,128)(2,1)S(1)}, u32[]{:S(2)}, u32[]{:S(2)}) collective-permute-start(bf16[1,2,2,48,576]{4,3,2,1,0:T(8,128)(2,1)S(1)} %copy.104), channel_id=1, source_target_pairs={{0,4},{1,5},{2,6},{3,7},{4,0},{5,1},{6,2},{7,3},{8,12},{9,13},{10,... | collective-permute-start | bytes 663560 | tf_op jit(solution)/shard_map/ppermute | solution.py:448
  492.8 70.7 %collective-permute-start.37 = (bf16[2,2,1,216,768]{4,3,2,1,0:T(8,128)(2,1)}, bf16[2,2,1,216,768]{4,3,2,1,0:T(8,128)(2,1)}, u32[]{:S(2)}, u32[]{:S(2)}) collective-permute-start(bf16[2,2,1,216,768]{4,3,2,1,0:T(8,128)(2,1)} %broadcast_select_fusion.2), channel_id=1, source_target_pairs={{0,1},{1,0},{2,3},{3,2},{4,5},{5,4},{6,7},{7,6},{8,9},{9,8},{10,11... | collective-permute-start | bytes 3981320 | tf_op jit(solution)/shard_map/ppermute | solution.py:448
  493.9 62.9 %collective-permute-start.32 = (bf16[1,48,576]{2,1,0:T(8,128)(2,1)S(1)}, bf16[1,48,576]{2,1,0:T(8,128)(2,1)S(1)}, u32[]{:S(2)}, u32[]{:S(2)}) collective-permute-start(bf16[1,48,576]{2,1,0:T(8,128)(2,1)S(1)} %select_bitcast_fusion.2), channel_id=1, source_target_pairs={{0,1},{1,0},{2,3},{3,2},{4,5},{5,4},{6,7},{7,6},{8,9},{9,8},{10,11... | collective-permute-start | bytes 165896 | tf_op jit(solution)/shard_map/ppermute | solution.py:448
  566.5 31.4 %collective-permute-start.38 = (bf16[1,2,1,216,768]{4,3,2,1,0:T(8,128)(2,1)S(1)}, bf16[1,2,1,216,768]{4,3,2,1,0:T(8,128)(2,1)S(1)}, u32[]{:S(2)}, u32[]{:S(2)}) collective-permute-start(bf16[1,2,1,216,768]{4,3,2,1,0:T(8,128)(2,1)S(1)} %broadcast_select_fusion.4), channel_id=1, source_target_pairs={{0,4},{1,5},{2,6},{3,7},{4,0},{5,1},{6,2},{7,3},{8,12},{9,13},{10,... | collective-permute-start | bytes 1990664 | tf_op jit(solution)/shard_map/ppermute | solution.py:448
  599.3 13.9 %collective-permute-start.25 = (bf16[384,768]{1,0:T(8,128)(2,1)}, bf16[384,768]{1,0:T(8,128)(2,1)S(1)}, u32[]{:S(2)}, u32[]{:S(2)}) collective-permute-start(bf16[384,768]{1,0:T(8,128)(2,1)} %get-tuple-element.47), channel_id=1, source_target_pairs={{0,1},{1,0},{2,3},{3,2},{4,5},{5,4},{6,7},{7,6},{8,9},{9,8},{10,11... | collective-permute-start | bytes 1769480 | tf_op jit(solution)/shard_map/ppermute | solution.py:448
  600.2 25.7 %collective-permute-start.27 = (bf16[384,768]{1,0:T(8,128)(2,1)}, bf16[384,768]{1,0:T(8,128)(2,1)}, u32[]{:S(2)}, u32[]{:S(2)}) collective-permute-start(bf16[384,768]{1,0:T(8,128)(2,1)} %get-tuple-element.48), channel_id=1, source_target_pairs={{0,1},{1,0},{2,3},{3,2},{4,5},{5,4},{6,7},{7,6},{8,9},{9,8},{10,11... | collective-permute-start | bytes 1769480 | tf_op jit(solution)/shard_map/ppermute | solution.py:448
  606.5 28.7 %collective-permute-start.40 = (bf16[216,768]{1,0:T(8,128)(2,1)S(1)}, bf16[216,768]{1,0:T(8,128)(2,1)S(1)}, u32[]{:S(2)}, u32[]{:S(2)}) collective-permute-start(bf16[216,768]{1,0:T(8,128)(2,1)S(1)} %fusion.29), channel_id=1, source_target_pairs={{0,16},{1,17},{2,18},{3,19},{4,20},{5,21},{6,22},{7,23},{8,24},{9,... | collective-permute-start | bytes 995336 | tf_op jit(solution)/shard_map/ppermute | solution.py:448
  628.9 17.4 %collective-permute-start.28 = (bf16[384,768]{1,0:T(8,128)(2,1)}, bf16[384,768]{1,0:T(8,128)(2,1)}, u32[]{:S(2)}, u32[]{:S(2)}) collective-permute-start(bf16[384,768]{1,0:T(8,128)(2,1)} %get-tuple-element.46), channel_id=1, source_target_pairs={{0,2},{1,3},{2,0},{3,1},{4,10},{5,11},{6,8},{7,9},{8,6},{9,7},{10,... | collective-permute-start | bytes 1769480 | tf_op jit(solution)/shard_map/ppermute | solution.py:448
  632.9 27.0 %collective-permute-start.26 = (bf16[384,768]{1,0:T(8,128)(2,1)S(1)}, bf16[384,768]{1,0:T(8,128)(2,1)}, u32[]{:S(2)}, u32[]{:S(2)}) collective-permute-start(bf16[384,768]{1,0:T(8,128)(2,1)S(1)} %get-tuple-element.45), channel_id=1, source_target_pairs={{0,0},{1,1},{2,2},{3,3},{4,8},{5,9},{6,10},{7,11},{8,4},{9,5},{10,... | collective-permute-start | bytes 1769480 | tf_op jit(solution)/shard_map/ppermute | solution.py:448
  636.2 30.6 %collective-permute-start.41 = (bf16[432,768]{1,0:T(8,128)(2,1)}, bf16[432,768]{1,0:T(8,128)(2,1)}, u32[]{:S(2)}, u32[]{:S(2)}) collective-permute-start(bf16[432,768]{1,0:T(8,128)(2,1)} %pad_maximum_fusion.10), channel_id=1, source_target_pairs={{0,8},{1,9},{2,10},{3,11},{4,12},{5,13},{6,14},{7,15},{8,0},{9,1},... | collective-permute-start | bytes 1990664 | tf_op jit(solution)/shard_map/ppermute | solution.py:448
  (66 other events, 527.9 us)
